TPU v7x, 512 devices: a whole 4x8x8 slice. The times are simulated.
512 devices in a mesh: video: 8 (over x, core), frame: 64 (over y, z).
Axes of the slice: x: 4, y: 8, z: 8, core: 2. Of those that a mesh axis runs over, the one named last changes fastest.
Arguments:
- tokens: bfloat16 [8, 128, 256, 1024], P('video', 'frame')
- counts: int32 [8], P('video'), may hold values from 2 to 128, as said below
- frame_index: int32 [8, 128], P('video'), may hold values from 0 to 127, each once within a row
- owner_slot: int32 [8, 128], P('video'), may hold values from 0 to 127, each once within a row
- gain_attn: float32 [1024], replicated
- gain_kv: float32 [1024], replicated, may hold values from 0.1 to 1.9
- slopes: float32 [16], replicated, may hold values from 0.003 to 0.15
- w_qkv: bfloat16 [1024, 3072], P('video', 'frame'), may hold values from -0.1875 to 0.1875
- w_out: bfloat16 [1024, 1024], P(None, 'video'), may hold values from -0.1875 to 0.1875
- w_kv: bfloat16 [1024, 2048], P(None, 'frame'), may hold values from -0.1875 to 0.1875
Outputs:
- res_keys: bfloat16 [8, 128, 256, 1024], P('video', 'frame')
- res_values: bfloat16 [8, 128, 256, 1024], P('video', 'frame')
Inputs may be any that keep to these rules, and one draw needn't show every extreme that they name: `frame_index`: each row is an ordering of frames 0 to 128 - 1 over a video's slots; frames at or past counts of that video are padding. `owner_slot`: each row is a permutation of the slots. `counts`: some video has all 128 frames.
All inputs are finite; a program needn't handle non-finite values.
Results may differ from a plain program's by a relative error of at most 0.0076.
Values may be sent and summed in bfloat16 or wider, within the bound.
A program may use at most 64 MiB of HBM per device.

v0:
```python
import jax
import jax.numpy as jnp
from jax import lax
from jax.sharding import PartitionSpec as P


def layer_norm(rows, gain):
    values = rows.astype(jnp.float32)
    center = jnp.mean(values, axis=-1, keepdims=True)
    spread = jnp.mean(jnp.square(values - center), axis=-1, keepdims=True)
    return ((values - center) * lax.rsqrt(spread + 1e-05) * gain).astype(jnp.bfloat16)


def project_qkv(rows, weight):
    width = rows.shape[3]
    flat = rows.reshape(-1, width)
    full_rows = lax.all_gather(weight, "video", axis=0, tiled=True)

    def apply_cols(piece, start):
        return jnp.dot(flat, piece, preferred_element_type=jnp.float32)

    result = apply_cols(lax.all_gather(full_rows, "frame", axis=1, tiled=True), jnp.int32(0))
    return result.astype(jnp.bfloat16).reshape(
        rows.shape[0], rows.shape[1], rows.shape[2], 3 * width
    )


def project_out(rows, weight):

    def apply_cols(piece, start):
        return jnp.dot(rows, piece, preferred_element_type=jnp.float32)

    return apply_cols(lax.all_gather(weight, "video", axis=1, tiled=True), jnp.int32(0))


def project_kv(rows, weight):

    def apply_cols(piece, start):
        return jnp.dot(rows, piece, preferred_element_type=jnp.float32)

    return apply_cols(lax.all_gather(weight, "frame", axis=1, tiled=True), jnp.int32(0))


def body(tokens, counts, frame_index, owner_slot, gain_attn, gain_kv, slopes, w_qkv, w_out, w_kv):
    groups = lax.axis_size("frame")
    my_index = lax.axis_index("frame")
    slots_dev = tokens.shape[1]
    patches = tokens.shape[2]
    width = tokens.shape[3]
    n_heads = slopes.shape[0]
    head_size = width // n_heads
    slots_all = slots_dev * groups
    pos_dev = patches // groups
    normed = layer_norm(tokens, gain_attn)
    qkv_local = project_qkv(normed, w_qkv)
    regrouped, qkv = (
        lax.all_to_all(tokens, "frame", split_axis=2, concat_axis=1, tiled=True),
        lax.all_to_all(qkv_local, "frame", split_axis=2, concat_axis=1, tiled=True),
    )
    query = qkv[0, :, :, :width].reshape(slots_all, pos_dev, n_heads, head_size)
    keyed = qkv[0, :, :, width : 2 * width].reshape(slots_all, pos_dev, n_heads, head_size)
    valued = qkv[0, :, :, 2 * width :].reshape(slots_all, pos_dev, n_heads, head_size)
    scores = jnp.einsum(
        "sphd,tphd->phst", query, keyed, preferred_element_type=jnp.float32
    ) * head_size ** (-0.5)
    frame_ids = frame_index[0]
    times = frame_ids.astype(jnp.float32)
    distance = jnp.abs(times[:, None] - times[None, :])
    scores = scores - slopes[None, :, None, None] * distance[None, None]
    valid = frame_ids < counts[0]
    scores = jnp.where(valid[None, None, None, :], scores, -1e30)
    top = jnp.max(scores, axis=-1, keepdims=True)
    expo = jnp.exp(scores - top)
    weights = (expo / jnp.sum(expo, axis=-1, keepdims=True)).astype(jnp.bfloat16)
    attended = jnp.einsum("phst,tphd->sphd", weights, valued, preferred_element_type=jnp.float32)
    attended = attended.astype(jnp.bfloat16).reshape(-1, width)
    updated = (
        regrouped.reshape(-1, width).astype(jnp.float32) + project_out(attended, w_out)
    ).astype(jnp.bfloat16)
    updated = updated.reshape(1, slots_all, pos_dev, width)
    inverse = (
        jnp.zeros((slots_all,), jnp.int32)
        .at[owner_slot[0]]
        .set(jnp.arange(slots_all, dtype=jnp.int32))
    )
    outgoing = jnp.take(updated, inverse, axis=1)
    arrived = lax.all_to_all(outgoing, "frame", split_axis=1, concat_axis=2, tiled=True)
    normed_kv = layer_norm(arrived, gain_kv).reshape(-1, width)
    pairs = (
        project_kv(normed_kv, w_kv).astype(jnp.bfloat16).reshape(1, slots_dev, patches, 2 * width)
    )
    sources = lax.dynamic_slice_in_dim(inverse, my_index * slots_dev, slots_dev)
    kept = jnp.take(frame_ids, sources) < counts[0]
    pairs = jnp.where(kept[None, :, None, None], pairs, jnp.zeros_like(pairs))
    return (pairs[..., :width], pairs[..., width:])


def solution(mesh):
    return jax.shard_map(
        body,
        mesh=mesh,
        in_specs=(
            P("video", "frame", None, None),
            P("video"),
            P("video", None),
            P("video", None),
            P(),
            P(),
            P(),
            P("video", "frame"),
            P(None, "video"),
            P(None, "frame"),
        ),
        out_specs=(P("video", "frame", None, None), P("video", "frame", None, None)),
        check_vma=False,
    )
```

profile of v0, /device:TPU:1, one launch (start us, length us, event | category | flops | bytes accessed | tf_op | source)
XLA Modules:
  0.0 337.3 jit_solution(8898248222884747381)
XLA Ops:
  7.2 0.0 all-gather.4.cloned.1.call-start
  7.2 19.0 %all_gather.12 = bf16[1024,48]{0,1:T(8,128)(2,1)} all-gather(bf16[128,48]{0,1:T(8,128)(2,1)} %param.17), channel_id=1, replica_groups=mesh['video'=8,'frame'=64] {'video'}, dimensions={0}, use_global_device_ids=true | all-gather | bytes 110592 | tf_op jit(solution)/shard_map/all_gather | solution.py:17
  26.2 0.0 all-gather.4.cloned.1.call-update
  26.2 0.0 copy-start.1
  26.2 3.4 copy.43
  29.6 12.0 %all-to-all-start = ((bf16[1,2,256,1024]{3,1,0,2:T(2,128)(2,1)}), bf16[1,2,256,1024]{3,1,0,2:T(2,128)(2,1)S(1)}, u32[]{:S(2)}, u32[]{:S(2)}) async-start(bf16[1,2,256,1024]{3,1,0,2:T(2,128)(2,1)} %copy.43), calls=%async_computation | async-start | bytes 2097152 | tf_op jit(solution)/shard_map/all_to_all | solution.py:57
  41.6 0.0 all-gather.6.cloned.1.call-start
  41.7 0.7 all-gather.6.cloned.1.call-update
  42.4 0.2 convert_reduce_fusion
  42.6 0.4 fusion.4
  43.0 0.0 copy-done.6
  43.0 0.4 fusion.6
  43.4 89.8 %all-gather.4.cloned.1.call-done = bf16[1024,3072]{0,1:T(8,128)(2,1)} async-done(((bf16[1024,48]{0,1:T(8,128)(2,1)}), bf16[1024,3072]{0,1:T(8,128)(2,1)}) %all-gather.4.cloned.1.call-update) | async-done | bytes 6291472 | tf_op jit(solution)/shard_map/all_gather | solution.py:22
  133.2 6.6 %convolution_convert_fusion = bf16[512,3072]{1,0:T(8,128)(2,1)S(1)} fusion(bf16[512,1024]{1,0:T(8,128)(2,1)S(1)} %bitcast.64, bf16[1024,3072]{0,1:T(8,128)(2,1)} %all-gather.4.cloned.1.call-done), kind=kOutput, calls=%fused_computation.4 | convolution fusion | flops 3222798336 | bytes 10485760 | tf_op jit(solution)/shard_map/dot_general | solution.py:20
  139.8 5.0 %copy.45 = bf16[1,2,256,3072]{3,1,0,2:T(2,128)(2,1)} copy(bf16[1,2,256,3072]{3,2,1,0:T(8,128)(2,1)S(1)} %bitcast.59) | data formatting | bytes 6291456 | tf_op jit(solution)/shard_map/reshape | solution.py:23
  144.7 0.0 all-to-all-done
  144.7 0.0 copy-start.2
  144.7 1.0 copy-done.2
  145.7 9.0 %all-to-all-start.1 = ((bf16[1,2,256,3072]{3,1,0,2:T(2,128)(2,1)}), bf16[1,2,256,3072]{3,1,0,2:T(2,128)(2,1)S(1)}, u32[]{:S(2)}, u32[]{:S(2)}) async-start(bf16[1,2,256,3072]{3,1,0,2:T(2,128)(2,1)} %copy.45), calls=%async_computation.1 | async-start | bytes 6291456 | tf_op jit(solution)/shard_map/all_to_all | solution.py:58
  154.7 0.0 all-gather.8.cloned.1.call-start
  154.7 0.7 all-gather.8.cloned.1.call-update
  156.1 1.2 scatter_custom_fusion
  157.3 0.1 subtract_abs_fusion
  157.4 0.0 copy-done.7
  157.4 1.1 broadcast_multiply_fusion
  158.5 3.3 copy.60
  161.8 3.0 reshape.233
  164.9 71.0 %all-to-all-done.1 = bf16[1,2,256,3072]{3,1,0,2:T(2,128)(2,1)S(1)} async-done(((bf16[1,2,256,3072]{3,1,0,2:T(2,128)(2,1)}), bf16[1,2,256,3072]{3,1,0,2:T(2,128)(2,1)S(1)}, u32[]{:S(2)}, u32[]{:S(2)}) %all-to-all-start.1) | async-done | bytes 3145760 | tf_op jit(solution)/shard_map/all_to_all | solution.py:58
  235.9 1.6 copy.46
  237.5 1.1 fusion.26
  238.6 1.7 copy.48
  240.3 1.7 copy.49
  242.0 1.7 copy.47
  243.7 5.2 %fusion.28 = (f32[4,16,128]{2,1,0:T(8,128)S(1)}, f32[4,16,128,128]{2,3,1,0:T(8,128)}) fusion(f32[16,128,128]{1,2,0:T(8,128)S(1)} %copy-done.3, pred[128]{0:T(512)(128)(4,1)S(1)} %broadcast_compare_fusion, bf16[128,4,16,64]{0,3,2,1:T(8,128)(2,1)S(1)} %bitcast.61, bf16[128,4,16,64]{0,3,2,1:T(8,128)(2,1)} %bitcast.62), kind=kOutput, calls=%fused_computation.60 | convolution fusion | flops 139460736 | bytes 7372928 | tf_op jit(solution)/shard_map/sub | solution.py:73
  248.9 2.9 fusion.13
  251.8 2.9 copy.51
  254.8 1.5 reshape.230
  256.2 0.0 all-gather.6.cloned.1.call-done
  256.3 3.5 %add_convert_fusion = bf16[512,1024]{1,0:T(8,128)(2,1)S(1)} fusion(f32[512,1024]{1,0:T(8,128)} %reshape.233, bf16[512,1024]{1,0:T(8,128)(2,1)S(1)} %reshape.230, bf16[1024,1024]{1,0:T(8,128)(2,1)} %all-gather.6.cloned.1.call-done), kind=kOutput, calls=%fused_computation.21 | convolution fusion | flops 1074790400 | bytes 6291456 | tf_op jit(solution)/shard_map/dot_general | solution.py:31
  259.8 0.4 reshape.246
  260.2 1.5 gather_fusion.1
  261.7 1.5 bitcast_select_fusion
  263.2 21.6 %all-to-all-start.2 = ((bf16[1,128,4,1024]{3,2,0,1:T(4,128)(2,1)}), bf16[1,128,4,1024]{3,2,0,1:T(4,128)(2,1)S(1)}, u32[]{:S(2)}, u32[]{:S(2)}) async-start(bf16[1,128,4,1024]{3,2,0,1:T(4,128)(2,1)} %bitcast_select_fusion), calls=%async_computation.2 | async-start | bytes 2097152 | tf_op jit(solution)/shard_map/all_to_all | solution.py:87
  284.8 0.1 compare_select_fusion.1
  284.9 0.6 gather_fusion
  285.5 0.1 fusion.21
  285.6 33.5 %all-to-all-done.2 = bf16[1,128,4,1024]{3,2,0,1:T(4,128)(2,1)S(1)} async-done(((bf16[1,128,4,1024]{3,2,0,1:T(4,128)(2,1)}), bf16[1,128,4,1024]{3,2,0,1:T(4,128)(2,1)S(1)}, u32[]{:S(2)}, u32[]{:S(2)}) %all-to-all-start.2) | async-done | bytes 1048608 | tf_op jit(solution)/shard_map/all_to_all | solution.py:87
  319.0 0.5 fusion.14
  319.6 0.1 copy.53
  319.7 0.1 copy.55
  319.8 0.1 copy.54
  319.9 0.9 multiply_reduce_fusion
  320.8 0.1 copy.56
  320.9 0.1 copy.57
  321.0 0.1 rsqrt.21
  321.2 0.1 div.27
  321.3 0.6 convert_bitcast_fusion
  321.9 0.2 copy.52
  322.1 0.0 copy-start.8
  322.1 1.8 reshape.234
  323.8 0.0 copy-done.8
  323.8 5.3 %convolution_convert_fusion.1 = bf16[512,2048]{1,0:T(8,128)(2,1)S(1)} fusion(bf16[1024,2048]{0,1:T(8,128)(2,1)} %all-gather.8.cloned.1.call-done, f32[512,1024]{1,0:T(8,128)} %reshape.234, f32[1024]{0:T(1024)S(1)} %copy-done.8, f32[512]{0:T(512)S(1)} %rsqrt.21, f32[512]{0:T(512)S(1)} %div.27), kind=kOutput, calls=%fused_computation.8 | convolution fusion | flops 2150629376 | bytes 8396800 | tf_op jit(solution)/shard_map/dot_general | solution.py:39
  329.1 0.2 broadcast_select_fusion
  329.3 1.5 fusion.27
  (26 shorter events, 0.1 us)
Async XLA Ops:
  7.2 126.0 %all-gather.4.cloned.1.call-start = ((), (), s32[]{:S(2)}) async-start(), calls=%async_computation.3 | async-start | bytes 6389760 | tf_op jit(solution)/shard_map/all_gather | solution.py:22
  26.2 16.2 %copy-start.1 = (bf16[1,2,256,1024]{3,2,1,0:T(8,128)(2,1)S(1)}, bf16[1,2,256,1024]{3,2,1,0:T(8,128)(2,1)}, u32[]{:S(2)}) copy-start(bf16[1,2,256,1024]{3,2,1,0:T(8,128)(2,1)} %param.10) | copy-start | bytes 3145732
  29.6 13.4 %copy-start.6 = (f32[1024]{0:T(1024)S(1)}, f32[1024]{0:T(1024)}, u32[]{:S(2)}) copy-start(f32[1024]{0:T(1024)} %param.14) | copy-start | bytes 12292
  29.6 115.1 %all-to-all-start = ((bf16[1,2,256,1024]{3,1,0,2:T(2,128)(2,1)}), bf16[1,2,256,1024]{3,1,0,2:T(2,128)(2,1)S(1)}, u32[]{:S(2)}, u32[]{:S(2)}) async-start(bf16[1,2,256,1024]{3,1,0,2:T(2,128)(2,1)} %copy.43), calls=%async_computation | async-start | bytes 2097152 | tf_op jit(solution)/shard_map/all_to_all | solution.py:57
  41.6 214.7 %all-gather.6.cloned.1.call-start = ((), (), s32[]{:S(2)}) async-start(), calls=%async_computation.4 | async-start | bytes 2359296 | tf_op jit(solution)/shard_map/all_gather | solution.py:33
  144.7 11.4 %copy-start.9 = (s32[1,128]{1,0:T(1,128)S(1)}, s32[1,128]{1,0:T(1,128)}, u32[]{:S(2)}) copy-start(s32[1,128]{1,0:T(1,128)} %param.13) | copy-start | bytes 1540
  144.7 12.6 %copy-start = (s32[1,128]{1,0:T(1,128)S(1)}, s32[1,128]{1,0:T(1,128)}, u32[]{:S(2)}) copy-start(s32[1,128]{1,0:T(1,128)} %param.12) | copy-start | bytes 1540
  144.7 12.7 %copy-start.7 = (f32[16]{0:T(128)S(1)}, f32[16]{0:T(128)}, u32[]{:S(2)}) copy-start(f32[16]{0:T(128)} %param.16) | copy-start | bytes 196
  144.7 1.0 copy-start.2
  145.7 90.2 %all-to-all-start.1 = ((bf16[1,2,256,3072]{3,1,0,2:T(2,128)(2,1)}), bf16[1,2,256,3072]{3,1,0,2:T(2,128)(2,1)S(1)}, u32[]{:S(2)}, u32[]{:S(2)}) async-start(bf16[1,2,256,3072]{3,1,0,2:T(2,128)(2,1)} %copy.45), calls=%async_computation.1 | async-start | bytes 6291456 | tf_op jit(solution)/shard_map/all_to_all | solution.py:58
  154.7 169.1 %all-gather.8.cloned.1.call-start = ((), (), s32[]{:S(2)}) async-start(), calls=%async_computation.5 | async-start | bytes 4259840 | tf_op jit(solution)/shard_map/all_gather | solution.py:41
  240.3 3.4 %copy-start.3 = (f32[16,128,128]{1,2,0:T(8,128)S(1)}, f32[16,128,128]{1,2,0:T(8,128)}, u32[]{:S(2)}) copy-start(f32[16,128,128]{1,2,0:T(8,128)} %broadcast_multiply_fusion) | copy-start | bytes 3145732
  242.0 1.7 copy-start.4
  243.7 5.2 %copy-start.5 = (bf16[1,128,4,1024]{1,3,2,0:T(8,128)(2,1)S(1)}, bf16[1,128,4,1024]{1,3,2,0:T(8,128)(2,1)}, u32[]{:S(2)}) copy-start(bf16[1,128,4,1024]{1,3,2,0:T(8,128)(2,1)} %copy.47) | copy-start | bytes 3145732
  263.2 55.8 %all-to-all-start.2 = ((bf16[1,128,4,1024]{3,2,0,1:T(4,128)(2,1)}), bf16[1,128,4,1024]{3,2,0,1:T(4,128)(2,1)S(1)}, u32[]{:S(2)}, u32[]{:S(2)}) async-start(bf16[1,128,4,1024]{3,2,0,1:T(4,128)(2,1)} %bitcast_select_fusion), calls=%async_computation.2 | async-start | bytes 2097152 | tf_op jit(solution)/shard_map/all_to_all | solution.py:87
  322.1 1.8 copy-start.8
Sparse Core Ops, SparseCore 0:
  26.3 106.8 all-gather.3
  135.3 30.3 all-gather.5
  168.7 146.2 all-gather.7
where the time goes:
time: 341 us; the launch traced here: 337 us
  waiting for transfers between devices  196 us (57%)
  starting transfers between devices  42.7 us (13%)
  local copies, waits for them, and re-layouts  35.6 us (10%)
  matrix products  23.5 us (7%)
  blocking collectives  19 us (6%)
  between operations  14.7 us (4%)
  other arithmetic  6.22 us (2%)
    all_gather x1, waiting for transfers between devices, project_qkv(): lax.all_gather(full_rows, 'frame', axis=1, tiled=True)  89.8 us
    all_to_all x1, waiting for transfers between devices, body(): lax.all_to_all(qkv_local, 'frame', split_axis=2, concat_axis=1, tiled=True)  71 us
    all_to_all x1, waiting for transfers between devices, body(): lax.all_to_all(outgoing, 'frame', split_axis=1, concat_axis=2, tiled=True)  33.5 us
    all_to_all x1, starting transfers between devices, body(): lax.all_to_all(outgoing, 'frame', split_axis=1, concat_axis=2, tiled=True)  21.6 us
    all_gather x1, blocking collectives, project_qkv(): full_rows = lax.all_gather(weight, 'video', axis=0, tiled=True)  19 us
    all_to_all x1, starting transfers between devices, body(): lax.all_to_all(tokens, 'frame', split_axis=2, concat_axis=1, tiled=True)  12 us
    all_to_all x1, starting transfers between devices, body(): lax.all_to_all(qkv_local, 'frame', split_axis=2, concat_axis=1, tiled=True)  8.97 us
    dot_general x2, matrix products, apply_cols(): return jnp.dot(rows, piece, preferred_element_type=jnp.float32)  8.76 us
  transfers between devices with their start and end apart: 6, of which 3 were waited for; matrix products, arithmetic and copies ran while one was open for 17% of the time, Pallas kernels for 0%

commit v1 on v0

--- a/solution.py
+++ b/solution.py
@@ -14,12 +14,11 @@
 def project_qkv(rows, weight):
     width = rows.shape[3]
     flat = rows.reshape(-1, width)
-    full_rows = lax.all_gather(weight, "video", axis=0, tiled=True)
-
-    def apply_cols(piece, start):
-        return jnp.dot(flat, piece, preferred_element_type=jnp.float32)
-
-    result = apply_cols(lax.all_gather(full_rows, "frame", axis=1, tiled=True), jnp.int32(0))
+    full_rows = lax.all_gather(weight.T, "video", axis=1, tiled=True)
+    piece = lax.all_gather(full_rows, "frame", axis=0, tiled=True)
+    result = lax.dot_general(
+        flat, piece, (((1,), (1,)), ((), ())), preferred_element_type=jnp.float32
+    )
     return result.astype(jnp.bfloat16).reshape(
         rows.shape[0], rows.shape[1], rows.shape[2], 3 * width
     )
@@ -35,10 +34,10 @@
 
 def project_kv(rows, weight):
 
-    def apply_cols(piece, start):
-        return jnp.dot(rows, piece, preferred_element_type=jnp.float32)
-
-    return apply_cols(lax.all_gather(weight, "frame", axis=1, tiled=True), jnp.int32(0))
+    piece = lax.all_gather(weight.T, "frame", axis=0, tiled=True)
+    return lax.dot_general(
+        rows, piece, (((1,), (1,)), ((), ())), preferred_element_type=jnp.float32
+    )
 
 
 def body(tokens, counts, frame_index, owner_slot, gain_attn, gain_kv, slopes, w_qkv, w_out, w_kv):
@@ -51,12 +50,8 @@
     head_size = width // n_heads
     slots_all = slots_dev * groups
     pos_dev = patches // groups
-    normed = layer_norm(tokens, gain_attn)
-    qkv_local = project_qkv(normed, w_qkv)
-    regrouped, qkv = (
-        lax.all_to_all(tokens, "frame", split_axis=2, concat_axis=1, tiled=True),
-        lax.all_to_all(qkv_local, "frame", split_axis=2, concat_axis=1, tiled=True),
-    )
+    regrouped = lax.all_to_all(tokens, "frame", split_axis=2, concat_axis=1, tiled=True)
+    qkv = project_qkv(layer_norm(regrouped, gain_attn), w_qkv)
     query = qkv[0, :, :, :width].reshape(slots_all, pos_dev, n_heads, head_size)
     keyed = qkv[0, :, :, width : 2 * width].reshape(slots_all, pos_dev, n_heads, head_size)
     valued = qkv[0, :, :, 2 * width :].reshape(slots_all, pos_dev, n_heads, head_size)

time: 341 us -> 287 us (0.84)
  waiting for transfers between devices: 196 us -> 159 us
  starting transfers between devices: 42.7 us -> 23.5 us
    all_to_all x1 -> x0, waiting for transfers between devices: 71 us -> none  [body(): lax.all_to_all(qkv_local, 'frame', split_axis=2, concat_axis=1, tiled=True)]
    all_to_all x1, waiting for transfers between devices: 0.01 us -> 26.5 us  [body(): lax.all_to_all(tokens, 'frame', split_axis=2, concat_axis=1, tiled=True)]
    all_gather x2, waiting for transfers between devices: 89.8 us -> 103 us  [the longest x1 52.3 us: project_qkv(): piece = lax.all_gather(full_rows, 'frame', axis=0, tiled=True)]
    all_to_all x1, starting transfers between devices: 21.6 us -> 11.5 us  [body(): lax.all_to_all(outgoing, 'frame', split_axis=1, concat_axis=2, tiled=True)]
    all_to_all x1 -> x0, starting transfers between devices: 8.97 us -> none  [body(): lax.all_to_all(qkv_local, 'frame', split_axis=2, concat_axis=1, tiled=True)]
    dot_general x1 -> x2, matrix products: 6.57 us -> 13.1 us  [the longest x1 7.88 us: project_qkv(): lax.dot_general(flat, piece, (((1,), (1,)), ((), ())), preferred_element_...]
    dot_general x2 -> x1, matrix products: 8.76 us -> 3.5 us  [apply_cols(): return jnp.dot(rows, piece, preferred_element_type=jnp.float32)]
    all_to_all x1, waiting for transfers between devices: 33.5 us -> 28.6 us  [body(): lax.all_to_all(outgoing, 'frame', split_axis=1, concat_axis=2, tiled=True)]
  transfers between devices with their start and end apart: 6 -> 5, of which waited for: 3 -> 4; matrix products, arithmetic and copies ran while one was open for 17% -> 21% of each run, Pallas kernels for 0% -> 0%
where the time goes in v1:
time: 287 us; the launch traced here: 283 us
  waiting for transfers between devices  159 us (55%)
  local copies, waits for them, and re-layouts  33.5 us (12%)
  matrix products  24.8 us (9%)
  starting transfers between devices  23.5 us (8%)
  blocking collectives  19 us (7%)
  between operations  14.7 us (5%)
  other arithmetic  8.2 us (3%)
    all_gather x1, waiting for transfers between devices, project_qkv(): piece = lax.all_gather(full_rows, 'frame', axis=0, tiled=True)  52.3 us
    all_gather x1, waiting for transfers between devices, project_kv(): piece = lax.all_gather(weight.T, 'frame', axis=0, tiled=True)  50.6 us
    all_to_all x1, waiting for transfers between devices, body(): lax.all_to_all(outgoing, 'frame', split_axis=1, concat_axis=2, tiled=True)  28.6 us
    all_to_all x1, waiting for transfers between devices, body(): lax.all_to_all(tokens, 'frame', split_axis=2, concat_axis=1, tiled=True)  26.5 us
    all_gather x1, blocking collectives, project_qkv(): full_rows = lax.all_gather(weight.T, 'video', axis=1, tiled=True)  19 us
    all_to_all x1, starting transfers between devices, body(): lax.all_to_all(tokens, 'frame', split_axis=2, concat_axis=1, tiled=True)  11.9 us
    all_to_all x1, starting transfers between devices, body(): lax.all_to_all(outgoing, 'frame', split_axis=1, concat_axis=2, tiled=True)  11.5 us
    dot_general x1, matrix products, project_qkv(): lax.dot_general(flat, piece, (((1,), (1,)), ((), ())), preferred_element_...  7.88 us
  transfers between devices with their start and end apart: 5, of which 4 were waited for; matrix products, arithmetic and copies ran while one was open for 21% of the time, Pallas kernels for 0%

profile of v1, /device:TPU:1, one launch (start us, length us, event | category | flops | bytes accessed | tf_op | source)
XLA Modules:
  0.0 283.0 jit_solution(18444236574860989863)
XLA Ops:
  7.2 0.0 all-gather.4.cloned.1.call-start
  7.2 19.0 %all_gather.12 = bf16[48,1024]{1,0:T(8,128)(2,1)} all-gather(bf16[48,128]{1,0:T(8,128)(2,1)} %bitcast.62), channel_id=1, replica_groups=mesh['video'=8,'frame'=64] {'video'}, dimensions={1}, use_global_device_ids=true | all-gather | bytes 110592 | tf_op jit(solution)/shard_map/all_gather | solution.py:17
  26.2 0.0 all-gather.4.cloned.1.call-update
  26.2 0.0 all-gather.6.cloned.1.call-start
  26.2 0.7 all-gather.6.cloned.1.call-update
  27.0 0.0 copy-start.10
  27.0 0.0 copy-start
  27.0 0.0 copy-start.7
  27.0 3.3 %copy.41 = bf16[1,2,256,1024]{3,1,0,2:T(2,128)(2,1)} copy(bf16[1,2,256,1024]{3,2,1,0:T(8,128)(2,1)} %param.10) | data formatting | bytes 2097152 | tf_op args[0]
  30.3 11.9 %all-to-all-start = ((bf16[1,2,256,1024]{3,1,0,2:T(2,128)(2,1)}), bf16[1,2,256,1024]{3,1,0,2:T(2,128)(2,1)S(1)}, u32[]{:S(2)}, u32[]{:S(2)}) async-start(bf16[1,2,256,1024]{3,1,0,2:T(2,128)(2,1)} %copy.41), calls=%async_computation | async-start | bytes 2097152 | tf_op jit(solution)/shard_map/all_to_all | solution.py:53
  42.2 0.0 all-gather.8.cloned.1.call-start
  42.2 0.7 all-gather.8.cloned.1.call-update
  42.9 0.0 copy-done.10
  42.9 1.0 scatter_custom_fusion
  44.6 0.1 subtract_abs_fusion
  44.7 1.2 broadcast_multiply_fusion
  45.9 26.5 %all-to-all-done = bf16[1,2,256,1024]{3,1,0,2:T(2,128)(2,1)S(1)} async-done(((bf16[1,2,256,1024]{3,1,0,2:T(2,128)(2,1)}), bf16[1,2,256,1024]{3,1,0,2:T(2,128)(2,1)S(1)}, u32[]{:S(2)}, u32[]{:S(2)}) %all-to-all-start) | async-done | bytes 1048608 | tf_op jit(solution)/shard_map/all_to_all | solution.py:53
  72.4 0.9 convert.11
  73.2 2.0 copy.60
  75.2 1.0 fusion.24
  76.2 0.1 div.25
  76.3 1.1 multiply_reduce_fusion.1
  77.4 0.1 rsqrt.23
  77.6 2.2 reshape.264
  79.7 0.0 copy-start.3
  79.7 52.3 %all-gather.4.cloned.1.call-done = bf16[3072,1024]{1,0:T(8,128)(2,1)} async-done(((bf16[48,1024]{1,0:T(8,128)(2,1)}), bf16[3072,1024]{1,0:T(8,128)(2,1)}) %all-gather.4.cloned.1.call-update) | async-done | bytes 6291472 | tf_op jit(solution)/shard_map/all_gather | solution.py:18
  132.0 0.0 copy-done.3
  132.0 7.9 %convolution_convert_fusion = bf16[512,3072]{1,0:T(8,128)(2,1)} fusion(bf16[3072,1024]{1,0:T(8,128)(2,1)} %all-gather.4.cloned.1.call-done, f32[512,1024]{1,0:T(8,128)S(1)} %reshape.264, f32[1024]{0:T(1024)S(1)} %copy-done.8, f32[512]{0:T(512)S(1)} %rsqrt.23, f32[512]{0:T(512)S(1)} %div.25), kind=kOutput, calls=%fused_computation.4 | convolution fusion | flops 3224895488 | bytes 11542528 | tf_op jit(solution)/shard_map/dot_general | solution.py:19
  139.9 4.8 %reshape.260 = bf16[1,128,4,3072]{3,2,1,0:T(4,128)(2,1)S(1)} reshape(bf16[512,3072]{1,0:T(8,128)(2,1)} %convolution_convert_fusion) | data formatting | bytes 6291456 | tf_op jit(solution)/shard_map/reshape | solution.py:22
  144.7 2.4 fusion.25
  147.2 2.8 copy.44
  150.0 1.7 copy.45
  151.7 1.7 copy.43
  153.4 5.2 %fusion.27 = (f32[4,16,128]{2,1,0:T(8,128)S(1)}, f32[4,16,128,128]{2,3,1,0:T(8,128)}) fusion(f32[16,128,128]{1,2,0:T(8,128)S(1)} %copy-done.4, pred[128]{0:T(512)(128)(4,1)S(1)} %broadcast_compare_fusion, bf16[128,4,16,64]{0,3,2,1:T(8,128)(2,1)S(1)} %bitcast.58, bf16[128,4,16,64]{0,3,2,1:T(8,128)(2,1)} %bitcast.59), kind=kOutput, calls=%fused_computation.59 | convolution fusion | flops 139460736 | bytes 7372928 | tf_op jit(solution)/shard_map/sub | solution.py:68
  158.5 3.0 %fusion.8 = bf16[128,4,16,64]{0,3,2,1:T(8,128)(2,1)S(1)} fusion(bf16[128,4,16,64]{0,3,2,1:T(8,128)(2,1)S(1)} %bitcast.60, f32[4,16,128,128]{2,3,1,0:T(8,128)} %get-tuple-element.10, f32[4,16,128]{2,1,0:T(8,128)S(1)} %get-tuple-element.9), kind=kOutput, calls=%fused_computation.24 | convolution fusion | flops 136839168 | bytes 6324224 | tf_op jit(solution)/shard_map/phst,tphd->sphd/dot_general | solution.py:70
  161.5 3.0 %copy.47 = bf16[128,4,16,64]{3,2,1,0:T(8,128)(2,1)S(1)} copy(bf16[128,4,16,64]{0,3,2,1:T(8,128)(2,1)S(1)} %fusion.8) | data formatting | bytes 2097152 | tf_op jit(solution)/shard_map/convert_element_type | solution.py:71
  164.5 1.5 reshape.261
  166.0 0.0 all-gather.6.cloned.1.call-done
  166.0 3.5 %add_convert_fusion = bf16[512,1024]{1,0:T(8,128)(2,1)S(1)} fusion(f32[512,1024]{1,0:T(8,128)} %copy-done.3, bf16[512,1024]{1,0:T(8,128)(2,1)S(1)} %reshape.261, bf16[1024,1024]{1,0:T(8,128)(2,1)} %all-gather.6.cloned.1.call-done), kind=kOutput, calls=%fused_computation.14 | convolution fusion | flops 1074790400 | bytes 6291456 | tf_op jit(solution)/shard_map/dot_general | solution.py:30
  169.5 0.7 reshape.278
  170.2 1.5 gather_fusion.1
  171.6 1.5 bitcast_select_fusion
  173.2 11.5 %all-to-all-start.1 = ((bf16[1,128,4,1024]{3,2,0,1:T(4,128)(2,1)}), bf16[1,128,4,1024]{3,2,0,1:T(4,128)(2,1)S(1)}, u32[]{:S(2)}, u32[]{:S(2)}) async-start(bf16[1,128,4,1024]{3,2,0,1:T(4,128)(2,1)} %bitcast_select_fusion), calls=%async_computation.1 | async-start | bytes 2097152 | tf_op jit(solution)/shard_map/all_to_all | solution.py:82
  184.7 0.1 compare_select_fusion.1
  184.8 0.6 gather_fusion
  185.4 0.1 fusion.19
  185.5 28.6 %all-to-all-done.1 = bf16[1,128,4,1024]{3,2,0,1:T(4,128)(2,1)S(1)} async-done(((bf16[1,128,4,1024]{3,2,0,1:T(4,128)(2,1)}), bf16[1,128,4,1024]{3,2,0,1:T(4,128)(2,1)S(1)}, u32[]{:S(2)}, u32[]{:S(2)}) %all-to-all-start.1) | async-done | bytes 1048608 | tf_op jit(solution)/shard_map/all_to_all | solution.py:82
  214.1 0.5 fusion.9
  214.6 0.1 copy.49
  214.7 0.1 copy.51
  214.8 0.1 copy.50
  214.9 0.9 multiply_reduce_fusion
  215.8 0.1 copy.52
  215.9 0.1 copy.53
  216.1 0.1 rsqrt.25
  216.2 0.1 div.30
  216.3 0.6 convert_bitcast_fusion
  216.9 0.2 copy.48
  217.1 0.0 copy-start.9
  217.1 1.8 reshape.265
  218.9 50.6 %all-gather.8.cloned.1.call-done = bf16[2048,1024]{1,0:T(8,128)(2,1)} async-done(((bf16[32,1024]{1,0:T(8,128)(2,1)}), bf16[2048,1024]{1,0:T(8,128)(2,1)}) %all-gather.8.cloned.1.call-update) | async-done | bytes 4194320 | tf_op jit(solution)/shard_map/all_gather | solution.py:37
  269.5 5.3 %convolution_convert_fusion.1 = bf16[512,2048]{1,0:T(8,128)(2,1)S(1)} fusion(bf16[2048,1024]{1,0:T(8,128)(2,1)} %all-gather.8.cloned.1.call-done, f32[512,1024]{1,0:T(8,128)} %reshape.265, f32[1024]{0:T(1024)S(1)} %copy-done.9, f32[512]{0:T(512)S(1)} %rsqrt.25, f32[512]{0:T(512)S(1)} %div.30), kind=kOutput, calls=%fused_computation.8 | convolution fusion | flops 2150629376 | bytes 8396800 | tf_op jit(solution)/shard_map/dot_general | solution.py:38
  274.8 0.2 broadcast_select_fusion
  275.0 1.5 fusion.26
  (27 shorter events, 0.2 us)
Async XLA Ops:
  7.2 124.9 %all-gather.4.cloned.1.call-start = ((), (), s32[]{:S(2)}) async-start(), calls=%async_computation.2 | async-start | bytes 6389760 | tf_op jit(solution)/shard_map/all_gather | solution.py:18
  26.2 139.8 %all-gather.6.cloned.1.call-start = ((), (), s32[]{:S(2)}) async-start(), calls=%async_computation.3 | async-start | bytes 2359296 | tf_op jit(solution)/shard_map/all_gather | solution.py:32
  27.0 16.0 %copy-start.10 = (s32[1,128]{1,0:T(1,128)S(1)}, s32[1,128]{1,0:T(1,128)}, u32[]{:S(2)}) copy-start(s32[1,128]{1,0:T(1,128)} %param.13) | copy-start | bytes 1540
  27.0 17.7 %copy-start = (s32[1,128]{1,0:T(1,128)S(1)}, s32[1,128]{1,0:T(1,128)}, u32[]{:S(2)}) copy-start(s32[1,128]{1,0:T(1,128)} %param.12) | copy-start | bytes 1540
  27.0 17.8 %copy-start.7 = (f32[16]{0:T(128)S(1)}, f32[16]{0:T(128)}, u32[]{:S(2)}) copy-start(f32[16]{0:T(128)} %param.16) | copy-start | bytes 196
  30.3 42.1 %all-to-all-start = ((bf16[1,2,256,1024]{3,1,0,2:T(2,128)(2,1)}), bf16[1,2,256,1024]{3,1,0,2:T(2,128)(2,1)S(1)}, u32[]{:S(2)}, u32[]{:S(2)}) async-start(bf16[1,2,256,1024]{3,1,0,2:T(2,128)(2,1)} %copy.41), calls=%async_computation | async-start | bytes 2097152 | tf_op jit(solution)/shard_map/all_to_all | solution.py:53
  42.2 227.3 %all-gather.8.cloned.1.call-start = ((), (), s32[]{:S(2)}) async-start(), calls=%async_computation.4 | async-start | bytes 4259840 | tf_op jit(solution)/shard_map/all_gather | solution.py:37
  77.6 54.5 %copy-start.8 = (f32[1024]{0:T(1024)S(1)}, f32[1024]{0:T(1024)}, u32[]{:S(2)}) copy-start(f32[1024]{0:T(1024)} %param.14) | copy-start | bytes 12292
  79.7 52.3 %copy-start.3 = (f32[512,1024]{1,0:T(8,128)}, f32[512,1024]{1,0:T(8,128)S(1)}, u32[]{:S(2)}) copy-start(f32[512,1024]{1,0:T(8,128)S(1)} %reshape.264) | copy-start | bytes 6291460
  147.2 2.8 copy-start.2
  147.2 4.5 %copy-start.1 = (bf16[1,128,4,1024]{3,2,1,0:T(4,128)(2,1)S(1)}, bf16[1,128,4,1024]{3,2,1,0:T(4,128)(2,1)}, u32[]{:S(2)}) copy-start(bf16[1,128,4,1024]{3,2,1,0:T(4,128)(2,1)} %get-tuple-element.4) | copy-start | bytes 3145732
  150.0 3.4 %copy-start.4 = (f32[16,128,128]{1,2,0:T(8,128)S(1)}, f32[16,128,128]{1,2,0:T(8,128)}, u32[]{:S(2)}) copy-start(f32[16,128,128]{1,2,0:T(8,128)} %broadcast_multiply_fusion) | copy-start | bytes 3145732
  151.7 1.7 copy-start.5
  153.3 5.2 %copy-start.6 = (bf16[1,128,4,1024]{1,3,2,0:T(8,128)(2,1)S(1)}, bf16[1,128,4,1024]{1,3,2,0:T(8,128)(2,1)}, u32[]{:S(2)}) copy-start(bf16[1,128,4,1024]{1,3,2,0:T(8,128)(2,1)} %copy.43) | copy-start | bytes 3145732
  173.2 40.9 %all-to-all-start.1 = ((bf16[1,128,4,1024]{3,2,0,1:T(4,128)(2,1)}), bf16[1,128,4,1024]{3,2,0,1:T(4,128)(2,1)S(1)}, u32[]{:S(2)}, u32[]{:S(2)}) async-start(bf16[1,128,4,1024]{3,2,0,1:T(4,128)(2,1)} %bitcast_select_fusion), calls=%async_computation.1 | async-start | bytes 2097152 | tf_op jit(solution)/shard_map/all_to_all | solution.py:82
  217.1 52.4 %copy-start.9 = (f32[1024]{0:T(1024)S(1)}, f32[1024]{0:T(1024)}, u32[]{:S(2)}) copy-start(f32[1024]{0:T(1024)} %param.15) | copy-start | bytes 12292
Sparse Core Ops, SparseCore 0:
  26.3 105.6 all-gather.3
  134.1 30.2 all-gather.5
  167.5 101.9 all-gather.7

commit v2 on v1

v2 whole, which is shorter than its diff:
```python
import functools
import jax
import jax.numpy as jnp
from jax import lax
from jax.experimental import pallas as pl
from jax.experimental.pallas import tpu as pltpu
from jax.sharding import PartitionSpec as P

XD, YD, ZD = 4, 8, 8
FRAMES = YD * ZD
SLOTS = 2 * FRAMES
POS = 4
ROWS = POS * SLOTS
D = 1024
HEADS = 16
MESH = pl.DeviceIdType.MESH
NT = (((1,), (1,)), ((), ()))
F32 = jnp.float32
BF16 = jnp.bfloat16


def lanes(block):
    return pl.ds(pl.multiple_of(block * 128, 128), 128)


def rows_at(start, count):
    return pl.ds(pl.multiple_of(start, count), count)


def norm(values, gain):
    center = jnp.mean(values, axis=-1, keepdims=True)
    shifted = values - center
    spread = jnp.mean(jnp.square(shifted), axis=-1, keepdims=True)
    return (shifted * lax.rsqrt(spread + 1e-05) * gain).astype(BF16)


def one_hot(rows, row_of_column):
    return jnp.where(rows == row_of_column, 1.0, 0.0).astype(BF16)


def kernel(
    tok, wq_mine, wk_mine, wo_mine, counts, frame_ids, owners, gain1, gain2, slopes,
    keys_out, values_out,
    wq, wk, wo, tx1, rx1, tx2, rx2, held, resid, normed, qkv, attended, updated, bias,
    s_weights, r_weights, s_plane, r_plane, s_tokens, r_tokens,
):
    v = lax.axis_index("video")
    f = lax.axis_index("frame")
    x, c = v // 2, v % 2
    y, z = f // ZD, f % ZD
    x_next, x_prev, x_far = (x + 1) % XD, (x + 3) % XD, (x + 2) % XD
    v_next, v_prev, v_far = 2 * x_next + c, 2 * x_prev + c, 2 * x_far + c
    v_twin = 2 * x + 1 - c

    def remote(src, dst, send, recv, device):
        return pltpu.make_async_remote_copy(
            src_ref=src, dst_ref=dst, send_sem=send, recv_sem=recv,
            device_id=device, device_id_type=MESH,
        )

    def plane_partner(i):
        return ((y + i // ZD) % YD) * ZD + (z + i % ZD) % ZD

    barrier = pltpu.get_barrier_semaphore()

    def greet(i, carry):
        pl.semaphore_signal(barrier, inc=1, device_id=(v, plane_partner(i)), device_id_type=MESH)
        return carry

    lax.fori_loop(1, FRAMES, greet, 0)
    for other in (v_next, v_prev, v_twin):
        pl.semaphore_signal(barrier, inc=1, device_id=(other, f), device_id_type=MESH)

    wq[y, z, :, lanes(v)] = wq_mine[...]
    wk[y, z, :, lanes(v)] = wk_mine[...]
    wo[:, lanes(v)] = wo_mine[...]
    low = lax.broadcasted_iota(jnp.int32, (8, 8, D), 1) < 4

    def lay_out(i, carry):
        first = tok[0, rows_at(64 * i, 64), :].astype(F32).reshape(8, 8, D)
        second = tok[1, rows_at(64 * i, 64), :].astype(F32).reshape(8, 8, D)
        even = jnp.where(low, first, pltpu.roll(second, 4, 1))
        odd = jnp.where(low, pltpu.roll(first, 4, 1), second)
        both = jnp.stack([even, odd], axis=1).reshape(16, 8, D)
        halves = jnp.concatenate([both[:, :, :512], both[:, :, 512:]], axis=1)
        tx1[rows_at(16 * i, 16)] = halves.astype(BF16)
        return carry

    lax.fori_loop(0, 4, lay_out, 0)
    rx1[f] = tx1[f]
    pl.semaphore_wait(barrier, FRAMES - 1 + 3)

    groups = {
        "q": (0, lambda half, block: wq.at[pl.ds(4 * half, 4), :, :, lanes(block)]),
        "o": (1, lambda half, block: wo.at[pl.ds(512 * half, 512), lanes(block)]),
        "k": (2, lambda half, block: wk.at[pl.ds(4 * half, 4), :, :, lanes(block)]),
    }
    moves = [
        (0, v, v_prev, v_next), (1, v, v_prev, v_next),
        (0, v, v_next, v_prev), (1, v, v_next, v_prev),
        (0, v_prev, v_far, v_next), (1, v_next, v_far, v_prev),
        (0, v, v_twin, v_twin), (1, v, v_twin, v_twin),
        (0, v_prev, 2 * x_prev + 1 - c, v_twin), (1, v_prev, 2 * x_prev + 1 - c, v_twin),
        (0, v_next, 2 * x_next + 1 - c, v_twin), (1, v_next, 2 * x_next + 1 - c, v_twin),
        (0, v_far, 2 * x_far + 1 - c, v_twin), (1, v_far, 2 * x_far + 1 - c, v_twin),
    ]

    def move(name, number):
        group, view = groups[name]
        half, block, _, target = moves[number]
        return remote(
            view(half, block), view(half, block),
            s_weights.at[group, number], r_weights.at[group, number], (target, f),
        )

    def start(name, *numbers):
        for number in numbers:
            move(name, number).start()

    def arrive(name, *numbers):
        group, view = groups[name]
        for number in numbers:
            half, _, block, target = moves[number]
            remote(
                view(half, block), view(half, block),
                s_weights.at[group, number], r_weights.at[group, number], (target, f),
            ).wait_recv()

    def own_moves(name):
        start(name, 0, 3, 1, 2, 6, 7)

    def forward_moves(name):
        arrive(name, 0)
        start(name, 4, 8)
        arrive(name, 3)
        start(name, 5, 11)
        arrive(name, 1)
        start(name, 9)
        arrive(name, 2)
        start(name, 10)

    def far_moves(name):
        arrive(name, 4)
        start(name, 12)
        arrive(name, 5)
        start(name, 13)

    def twin_moves(name):
        arrive(name, *range(6, 14))

    def plane_z(ref, mine, number):
        def send(i, carry):
            here = ref.at[y, z, :, lanes(v)]
            remote(mine, here, s_plane.at[number], r_plane.at[number],
                   (v, y * ZD + (z + i) % ZD)).start()
            return carry
        lax.fori_loop(1, ZD, send, 0)

    def plane_z_wait(ref, number):
        span = ref.at[0, pl.ds(0, ZD - 1), :, lanes(v)]
        remote(span, span, s_plane.at[number], r_plane.at[number], (v, f)).wait_recv()

    def plane_y(ref, number):
        def send(i, carry):
            here = ref.at[y, :, :, lanes(v)]
            remote(here, here, s_plane.at[number], r_plane.at[number],
                   (v, ((y + i) % YD) * ZD + z)).start()
            return carry
        lax.fori_loop(1, YD, send, 0)

    def plane_y_wait(ref, number):
        span = ref.at[pl.ds(0, YD - 1), :, :, lanes(v)]
        remote(span, span, s_plane.at[number], r_plane.at[number], (v, f)).wait_recv()

    def exchange(src, dst, number):
        def send(i, carry):
            g = plane_partner(i)
            remote(src.at[g], dst.at[f], s_tokens.at[number], r_tokens.at[number], (v, g)).start()
            return carry
        lax.fori_loop(1, FRAMES, send, 0)

    def exchange_wait(dst, number):
        span = dst.at[pl.ds(0, FRAMES - 1)]
        remote(span, span, s_tokens.at[number], r_tokens.at[number], (v, f)).wait_recv()

    own_moves("o")
    plane_z(wq, wq_mine, 0)
    plane_z(wk, wk_mine, 2)
    plane_z_wait(wq, 0)
    plane_y(wq, 1)
    exchange(tx1, rx1, 0)
    plane_y_wait(wq, 1)
    own_moves("q")
    plane_z_wait(wk, 2)
    plane_y(wk, 3)
    forward_moves("o")
    far_moves("o")
    forward_moves("q")

    slot_row = owners[...]
    frame_row = frame_ids[...].astype(F32)
    sub = lax.broadcasted_iota(jnp.int32, (SLOTS, SLOTS), 0)
    lane = lax.broadcasted_iota(jnp.int32, (SLOTS, SLOTS), 1)
    place = jnp.where(sub == slot_row, 1.0, 0.0)
    time_col = jnp.sum(place * frame_row, axis=1, keepdims=True)
    time_row = jnp.sum(jnp.where(sub == lane, time_col, 0.0), axis=0, keepdims=True)
    count = counts[0].astype(F32)
    distance = jnp.abs(time_col - time_row)
    valid = time_row < count

    def head_bias(h, carry):
        bias[h] = jnp.where(valid, -slopes[h] * distance, -1e30)
        return carry

    lax.fori_loop(0, HEADS, head_bias, 0)
    row_pos = lax.broadcasted_iota(jnp.int32, (SLOTS, ROWS), 1)
    spread = jnp.where(
        row_pos // POS == lax.broadcasted_iota(jnp.int32, (SLOTS, ROWS), 0), 1.0, 0.0
    )
    slot_col = jnp.sum(
        jnp.where(sub == lane, slot_row.astype(F32), 0.0), axis=1, keepdims=True
    )
    target = jnp.sum(spread * slot_col, axis=0, keepdims=True).astype(jnp.int32)
    target = target + (lax.broadcasted_iota(jnp.int32, (1, ROWS), 1) % POS) * SLOTS

    exchange_wait(rx1, 0)

    def unpack(i, carry):
        blocks = rx1[rows_at(8 * i, 8)].astype(F32)
        held[rows_at(64 * i, 64), :512] = blocks[:, :8].reshape(64, 512).astype(BF16)
        held[rows_at(64 * i, 64), 512:] = blocks[:, 8:].reshape(64, 512).astype(BF16)
        return carry

    lax.fori_loop(0, 8, unpack, 0)
    out_row = lax.broadcasted_iota(jnp.int32, (SLOTS, ROWS), 0)

    def place_and_norm(p, carry):
        picked = jnp.dot(
            one_hot(out_row + p * SLOTS, target), held[...], preferred_element_type=F32
        )
        resid[rows_at(SLOTS * p, SLOTS)] = picked.astype(BF16)
        normed[rows_at(SLOTS * p, SLOTS)] = norm(picked, gain1[...])
        return carry

    lax.fori_loop(0, POS, place_and_norm, 0)

    far_moves("q")
    plane_y_wait(wk, 3)
    own_moves("k")
    twin_moves("q")

    def project(j, carry):
        weight = wq[rows_at(2 * j, 2)].reshape(768, D)
        result = lax.dot_general(normed[...], weight, NT, preferred_element_type=F32)
        qkv[:, pl.ds(pl.multiple_of(768 * j, 128), 768)] = result.astype(BF16)
        return carry

    lax.fori_loop(0, 4, project, 0)
    forward_moves("k")

    left = lax.broadcasted_iota(jnp.int32, (SLOTS, 128), 1) < 64

    def attend(i, carry):
        p = i // 4
        here = rows_at(SLOTS * p, SLOTS)
        for j in range(2):
            pair = (i % 4) * 2 + j
            query = qkv[here, lanes(pair)]
            keyed = qkv[here, lanes(8 + pair)]
            valued = qkv[here, lanes(16 + pair)]
            parts = []
            for side in range(2):
                mine = left if side == 0 else jnp.logical_not(left)
                scores = lax.dot_general(
                    jnp.where(mine, query, jnp.zeros_like(query)), keyed, NT,
                    preferred_element_type=F32,
                )
                scores = scores * 0.125 + bias[2 * pair + side]
                expo = jnp.exp(scores - jnp.max(scores, axis=1, keepdims=True))
                weights = expo * (1.0 / jnp.sum(expo, axis=1, keepdims=True))
                parts.append(
                    jnp.dot(weights.astype(BF16), valued, preferred_element_type=F32)
                )
            attended[here, lanes(pair)] = jnp.where(left, parts[0], parts[1]).astype(BF16)
        return carry

    lax.fori_loop(0, 16, attend, 0)
    twin_moves("o")

    def project_out(p, carry):
        here = rows_at(SLOTS * p, SLOTS)
        added = jnp.dot(attended[here], wo[...], preferred_element_type=F32)
        updated[here] = (resid[here].astype(F32) + added).astype(BF16)
        return carry

    lax.fori_loop(0, POS, project_out, 0)

    out_col = lax.broadcasted_iota(jnp.int32, (128, ROWS), 1)
    out_row2 = lax.broadcasted_iota(jnp.int32, (128, ROWS), 0)

    def lay_out_updated(i, carry):
        row = out_row2 + 128 * i
        source = (row % 4) * SLOTS + 2 * (row // 8) + (row % 8) // 4
        moved = jnp.dot(one_hot(source, out_col), updated[...], preferred_element_type=F32)
        both = moved.reshape(16, 8, D)
        halves = jnp.concatenate([both[:, :, :512], both[:, :, 512:]], axis=1)
        tx2[rows_at(16 * i, 16)] = halves.astype(BF16)
        return carry

    lax.fori_loop(0, 4, lay_out_updated, 0)
    exchange(tx2, rx2, 1)
    rx2[f] = tx2[f]
    far_moves("k")
    twin_moves("k")
    exchange_wait(rx2, 1)

    def norm_arrived(i, carry):
        blocks = rx2[rows_at(16 * i, 16)].astype(F32)
        both = jnp.concatenate([blocks[:, :8], blocks[:, 8:]], axis=2).reshape(8, 2, 8, D)
        even, odd = both[:, 0], both[:, 1]
        first = jnp.where(low, even, pltpu.roll(odd, 4, 1)).reshape(64, D)
        second = jnp.where(low, pltpu.roll(even, 4, 1), odd).reshape(64, D)
        normed[rows_at(64 * i, 64)] = norm(first, gain2[...])
        normed[rows_at(256 + 64 * i, 64)] = norm(second, gain2[...])
        return carry

    lax.fori_loop(0, 4, norm_arrived, 0)

    lane_row = lax.broadcasted_iota(jnp.int32, (1, SLOTS), 1)
    kept = jnp.where(valid, 1.0, 0.0)
    kept_first = jnp.sum(jnp.where(lane_row == 2 * f, kept, 0.0), axis=1, keepdims=True)
    kept_second = jnp.sum(jnp.where(lane_row == 2 * f + 1, kept, 0.0), axis=1, keepdims=True)
    row_kept = jnp.where(
        lax.broadcasted_iota(jnp.int32, (ROWS, 1), 0) < 256, kept_first, kept_second
    ) > 0.5

    for j in range(4):
        weight = wk[pl.ds(2 * j, 2)].reshape(512, D)
        result = lax.dot_general(normed[...], weight, NT, preferred_element_type=F32)
        result = jnp.where(row_kept, result, 0.0).astype(BF16)
        out = keys_out if j < 2 else values_out
        out[:, pl.ds(512 * (j % 2), 512)] = result

    for name in groups:
        for number in range(len(moves)):
            move(name, number).wait_send()
    for number, ref in ((0, wq), (2, wk)):
        span = ref.at[0, pl.ds(0, ZD - 1), :, lanes(v)]
        remote(span, span, s_plane.at[number], r_plane.at[number], (v, f)).wait_send()
    for number, ref in ((1, wq), (3, wk)):
        span = ref.at[pl.ds(0, YD - 1), :, :, lanes(v)]
        remote(span, span, s_plane.at[number], r_plane.at[number], (v, f)).wait_send()
    for number, ref in ((0, rx1), (1, rx2)):
        span = ref.at[pl.ds(0, FRAMES - 1)]
        remote(span, span, s_tokens.at[number], r_tokens.at[number], (v, f)).wait_send()


def body(tokens, counts, frame_index, owner_slot, gain_attn, gain_kv, slopes, w_qkv, w_out, w_kv):
    v = lax.axis_index("video")
    wq_mine = w_qkv.T
    wk_mine = lax.dynamic_slice_in_dim(w_kv, v * 128, 128, 0).T
    vmem = pl.BlockSpec(memory_space=pltpu.VMEM)
    smem = pl.BlockSpec(memory_space=pltpu.SMEM)
    dma = pltpu.SemaphoreType.DMA
    keys, values = pl.pallas_call(
        kernel,
        out_shape=(
            jax.ShapeDtypeStruct((ROWS, D), BF16),
            jax.ShapeDtypeStruct((ROWS, D), BF16),
        ),
        in_specs=[vmem] * 4 + [smem] + [vmem] * 4 + [smem],
        out_specs=(vmem, vmem),
        scratch_shapes=[
            pltpu.VMEM((YD, ZD, 48, D), BF16),
            pltpu.VMEM((YD, ZD, 32, D), BF16),
            pltpu.VMEM((D, D), BF16),
            pltpu.VMEM((FRAMES, 16, 512), BF16),
            pltpu.VMEM((FRAMES, 16, 512), BF16),
            pltpu.VMEM((FRAMES, 16, 512), BF16),
            pltpu.VMEM((FRAMES, 16, 512), BF16),
            pltpu.VMEM((ROWS, D), BF16),
            pltpu.VMEM((ROWS, D), BF16),
            pltpu.VMEM((ROWS, D), BF16),
            pltpu.VMEM((ROWS, 3 * D), BF16),
            pltpu.VMEM((ROWS, D), BF16),
            pltpu.VMEM((ROWS, D), BF16),
            pltpu.VMEM((HEADS, SLOTS, SLOTS), F32),
            dma((3, 14)), dma((3, 14)), dma((4,)), dma((4,)), dma((2,)), dma((2,)),
        ],
        compiler_params=pltpu.CompilerParams(
            collective_id=0, has_side_effects=True, vmem_limit_bytes=60 * 2**20
        ),
    )(
        tokens[0], wq_mine, wk_mine, w_out, counts, frame_index, owner_slot,
        gain_attn.reshape(1, D), gain_kv.reshape(1, D), slopes,
    )
    return keys.reshape(1, 2, 256, D), values.reshape(1, 2, 256, D)


def solution(mesh):
    return jax.shard_map(
        body,
        mesh=mesh,
        in_specs=(
            P("video", "frame", None, None),
            P("video"),
            P("video", None),
            P("video", None),
            P(),
            P(),
            P(),
            P("video", "frame"),
            P(None, "video"),
            P(None, "frame"),
        ),
        out_specs=(P("video", "frame", None, None), P("video", "frame", None, None)),
        check_vma=False,
    )
```

time: 287 us -> 154 us (0.54)
  waiting for transfers between devices: 159 us -> 0 us
  Pallas kernels: 0 us -> 145 us
  local copies, waits for them, and re-layouts: 33.5 us -> 4.08 us
  matrix products: 24.8 us -> 0 us
  starting transfers between devices: 23.5 us -> 0 us
  blocking collectives: 19 us -> 0 us
  between operations: 14.7 us -> 1.34 us
  other arithmetic: 8.2 us -> 0 us
    pallas_call x0 -> x1, Pallas kernels: none -> 145 us  [body(): pl.pallas_call(kernel, out_shape=(jax.ShapeDtypeStruct((ROWS, D), BF16),...]
    all_gather x3 -> x0, waiting for transfers between devices: 103 us -> none  [the longest x1 52.3 us: project_qkv(): piece = lax.all_gather(full_rows, 'frame', axis=0, tiled=True)]
    all_to_all x2 -> x0, waiting for transfers between devices: 55.1 us -> none  [the longest x1 28.6 us: body(): lax.all_to_all(outgoing, 'frame', split_axis=1, concat_axis=2, tiled=True)]
    all_to_all x2 -> x0, starting transfers between devices: 23.4 us -> none  [the longest x1 11.9 us: body(): lax.all_to_all(tokens, 'frame', split_axis=2, concat_axis=1, tiled=True)]
    dot_general x4 -> x0, matrix products: 19.6 us -> none  [the longest x1 7.88 us: project_qkv(): lax.dot_general(flat, piece, (((1,), (1,)), ((), ())), preferred_element_...]
    all_gather x1 -> x0, blocking collectives: 19 us -> none  [project_qkv(): full_rows = lax.all_gather(weight.T, 'video', axis=1, tiled=True)]
    slice x5 -> x0, local copies, waits for them, and re-layouts: 10.1 us -> none  [the longest x2 4.1 us: body(): qkv[0, :, :, width:2 * width]]
    convert_element_type x5 -> x0, local copies, waits for them, and re-layouts: 9.05 us -> none  [the longest x2 4.11 us: body(): regrouped.reshape(-1, width).astype(jnp.float32)]
  transfers between devices with their start and end apart: 5 -> 0, of which waited for: 4 -> 0; matrix products, arithmetic and copies ran while one was open for 21% -> 0% of each run, Pallas kernels for 0% -> 0%
where the time goes in v2:
time: 154 us; the launch traced here: 151 us
  Pallas kernels  145 us (94%)
  local copies, waits for them, and re-layouts  4.08 us (3%)
    pallas_call x1, Pallas kernels, body(): pl.pallas_call(kernel, out_shape=(jax.ShapeDtypeStruct((ROWS, D), BF16),...  145 us
    unnamed x6, local copies, waits for them, and re-layouts  3.48 us

profile of v2, /device:TPU:1, one launch (start us, length us, event | category | flops | bytes accessed | tf_op | source)
XLA Modules:
  0.0 150.9 jit_solution(7613092462731733531)
XLA Ops:
  0.6 0.0 copy-start
  1.3 0.1 copy-done
  1.5 0.6 dynamic-slice_bitcast_fusion.wk_mine
  2.1 145.5 %shard_map.113 = (bf16[512,1024]{1,0:T(8,128)(2,1)}, bf16[512,1024]{1,0:T(8,128)(2,1)}) custom-call(bf16[2,256,1024]{2,1,0:T(8,128)(2,1)} %bitcast.8, bf16[48,128]{1,0:T(8,128)(2,1)} %bitcast.11, bf16[32,128]{1,0:T(8,128)(2,1)} %dynamic-slice_bitcast_fusion.wk_mine, bf16[1024,128]{1,0:T(8,128)(2,1)} %wo_mine.1, s32[1]{0:T(128)S(6)} %copy.14.counts, ...), custom_call_target="tpu_custom_call" | custom-call | tf_op jit(solution)/shard_map/pallas_call | solution.py:365
  147.6 0.0 copy-start.1
  147.6 2.4 %copy.15 = bf16[1,2,256,1024]{3,2,1,0:T(8,128)(2,1)} copy(bf16[1,2,256,1024]{3,2,1,0:T(8,128)(2,1)} %bitcast.10) | data formatting | bytes 2097152
  149.9 0.0 copy-done.1
  149.9 1.0 copy.16
Async XLA Ops:
  0.6 0.8 copy-start
  147.6 2.4 %copy-start.1 = (bf16[512,1024]{1,0:T(8,128)(2,1)S(1)}, bf16[512,1024]{1,0:T(8,128)(2,1)}, u32[]{:S(2)}) copy-start(bf16[512,1024]{1,0:T(8,128)(2,1)} %get-tuple-element.5) | copy-start | bytes 3145732

commit v3 on v2

v3 whole, which is shorter than its diff:
```python
import functools
import jax
import jax.numpy as jnp
from jax import lax
from jax.experimental import pallas as pl
from jax.experimental.pallas import tpu as pltpu
from jax.sharding import PartitionSpec as P

XD, YD, ZD = 4, 8, 8
FRAMES = YD * ZD
SLOTS = 2 * FRAMES
POS = 4
ROWS = POS * SLOTS
D = 1024
HEADS = 16
NEAR = (1, 7, 2, 6, 3, 5, 4)
MESH = pl.DeviceIdType.MESH
NT = (((1,), (1,)), ((), ()))
F32 = jnp.float32
BF16 = jnp.bfloat16


def lanes(block):
    return pl.ds(pl.multiple_of(block * 128, 128), 128)


def rows_at(start, count):
    return pl.ds(pl.multiple_of(start, count), count)


def norm(values, gain):
    center = jnp.mean(values, axis=-1, keepdims=True)
    shifted = values - center
    spread = jnp.mean(jnp.square(shifted), axis=-1, keepdims=True)
    return (shifted * lax.rsqrt(spread + 1e-05) * gain).astype(BF16)


def one_hot(rows, row_of_column):
    return jnp.where(rows == row_of_column, 1.0, 0.0).astype(BF16)


def kernel(
    tok, wq_mine, wk_mine, wo_mine, counts, frame_ids, owners, gain1, gain2, slopes,
    keys_out, values_out,
    wq, wk, wo, tx1, rx1, tx2, rx2, held, resid, normed, query_t, keyed, value_t,
    attended_t, bias, own_q, own_k,
    s_plane, r_plane, r_piece, s_span, r_span, s_tokens, r_tokens, row_in,
):
    v = lax.axis_index("video")
    f = lax.axis_index("frame")
    x, c = v // 2, v % 2
    y, z = f // ZD, f % ZD
    x_next, x_prev, x_far = (x + 1) % XD, (x + 3) % XD, (x + 2) % XD
    v_next, v_prev, v_far = 2 * x_next + c, 2 * x_prev + c, 2 * x_far + c
    v_twin = 2 * x + 1 - c

    def remote(src, dst, send, recv, device):
        return pltpu.make_async_remote_copy(
            src_ref=src, dst_ref=dst, send_sem=send, recv_sem=recv,
            device_id=device, device_id_type=MESH,
        )

    def along_y(i):
        return (v, ((y + i) % YD) * ZD + z)

    def along_z(i):
        return (v, y * ZD + (z + i) % ZD)

    barrier = pltpu.get_barrier_semaphore()
    for i in range(1, 8):
        for device in (along_y(i), along_z(i)):
            pl.semaphore_signal(barrier, inc=1, device_id=device, device_id_type=MESH)
    for other in (v_next, v_prev, v_twin):
        pl.semaphore_signal(barrier, inc=1, device_id=(other, f), device_id_type=MESH)

    own_q[...] = wq_mine[...]
    own_k[...] = wk_mine[:, lanes(v)]
    wq[y, z, :, lanes(v)] = own_q[...]
    wk[y, z, :, lanes(v)] = own_k[...]
    wo[:, lanes(v)] = wo_mine[...]
    low = lax.broadcasted_iota(jnp.int32, (8, 8, D), 1) < 4

    def lay_out(i, carry):
        first = tok[0, rows_at(64 * i, 64), :].astype(F32).reshape(8, 8, D)
        second = tok[1, rows_at(64 * i, 64), :].astype(F32).reshape(8, 8, D)
        even = jnp.where(low, first, pltpu.roll(second, 4, 1))
        odd = jnp.where(low, pltpu.roll(first, 4, 1), second)
        both = jnp.stack([even, odd], axis=1).reshape(16, 8, D)
        halves = jnp.concatenate([both[:, :, :512], both[:, :, 512:]], axis=1)
        tx1[rows_at(16 * i, 16)] = halves.astype(BF16)
        return carry

    lax.fori_loop(0, 4, lay_out, 0)
    rx1[f] = tx1[f]
    pl.semaphore_wait(barrier, 17)
    for i in NEAR:
        pl.semaphore_signal(row_in, inc=1, device_id=along_y(i), device_id_type=MESH)

    def q_piece(core, i, block):
        if core == 0:
            return wq.at[(y + i) % YD, :, :, lanes(block)]
        return wq.at[:, (z + i) % ZD, :, lanes(block)]

    def whole(ref, block):
        return ref.at[:, lanes(block)] if ref is wo else ref.at[:, :, :, lanes(block)]

    def half(ref, number, block):
        if ref is wo:
            return wo.at[pl.ds(512 * number, 512), lanes(block)]
        return ref.at[pl.ds(4 * number, 4), :, :, lanes(block)]

    def plane_first(core, ref, mine, number):
        here = ref.at[y, z, :, lanes(v)]
        for i in NEAR:
            remote(mine, here, s_plane.at[number], r_plane.at[number],
                   along_z(i) if core == 0 else along_y(i)).start()

    def seven(core, ref):
        if core == 0:
            return ref.at[0, pl.ds(0, 7), :, lanes(v)]
        return ref.at[pl.ds(0, 7), 0, :, lanes(v)]

    def plane_first_wait(core, ref, number):
        span = seven(core, ref)
        remote(span, span, s_plane.at[number], r_plane.at[number], (v, f)).wait_recv()

    def send_tokens(src, dst, number, to_y, to_z):
        g = to_y * ZD + to_z
        remote(src.at[g], dst.at[f], s_tokens.at[number], r_tokens.at[number], (v, g)).start()

    def tokens_wait(dst, number):
        span = dst.at[pl.ds(0, FRAMES - 1)]
        remote(span, span, s_tokens.at[number], r_tokens.at[number], (v, f)).wait_recv()

    groups = {"q": (0, wq), "o": (1, wo), "k": (2, wk)}
    moves = [
        (0, v, v_prev, v_next), (1, v, v_prev, v_next),
        (0, v, v_next, v_prev), (1, v, v_next, v_prev),
        (0, v_prev, v_far, v_next), (1, v_next, v_far, v_prev),
        (None, v, v_twin, v_twin),
        (None, v_prev, 2 * x_prev + 1 - c, v_twin),
        (None, v_next, 2 * x_next + 1 - c, v_twin),
        (0, v_far, 2 * x_far + 1 - c, v_twin), (1, v_far, 2 * x_far + 1 - c, v_twin),
    ]

    def view(name, part, block):
        ref = groups[name][1]
        return whole(ref, block) if part is None else half(ref, part, block)

    def move(name, number):
        group = groups[name][0]
        part, block, _, target = moves[number]
        here = view(name, part, block)
        return remote(here, here, s_span.at[group, number], r_span.at[group, number], (target, f))

    def start(name, *numbers):
        for number in numbers:
            move(name, number).start()

    def arrive(name, *numbers):
        group = groups[name][0]
        for number in numbers:
            part, _, block, target = moves[number]
            here = view(name, part, block)
            remote(
                here, here, s_span.at[group, number], r_span.at[group, number], (target, f)
            ).wait_recv()

    def own_moves(name):
        start(name, 0, 3, 1, 2, 6)

    def forward_moves(name):
        arrive(name, 0)
        start(name, 4)
        arrive(name, 3)
        start(name, 5)
        arrive(name, 1)
        start(name, 7)
        arrive(name, 2)
        start(name, 8)

    def far_moves(name):
        arrive(name, 4)
        start(name, 9)
        arrive(name, 5)
        start(name, 10)

    def twin_moves(name):
        arrive(name, 6, 7, 8, 9, 10)

    def gather(core):
        order = (0,) + NEAR
        plane_first(core, wq, own_q, 0)
        plane_first(core, wk, own_k, 1)
        own_moves("o")
        plane_first_wait(core, wq, 0)

        def send_x(position):
            i = -order[position] % 8
            here = q_piece(core, i, v)
            remote(here, here, s_span.at[0, 0], r_piece.at[1, position], (v_next, f)).start()
            remote(here, here, s_span.at[0, 1], r_piece.at[2, position], (v_prev, f)).start()

        def arrived(column, position, block):
            here = q_piece(core, -order[position] % 8, block)
            remote(here, here, s_span.at[0, 0], r_piece.at[column, position], (v, f)).wait_recv()

        def forward(position):
            arrived(1, position, v_prev)
            if position % 2 == 0:
                here = q_piece(core, -order[position] % 8, v_prev)
                remote(here, here, s_span.at[0, 2], r_piece.at[3, position], (v_next, f)).start()
            arrived(2, position, v_next)
            if position % 2 == 1:
                here = q_piece(core, -order[position] % 8, v_next)
                remote(here, here, s_span.at[0, 2], r_piece.at[3, position], (v_prev, f)).start()

        step = along_y if core == 0 else along_z

        def hand_on(position):
            i = order[position]
            here = q_piece(core, -i % 8, v)
            if position == 0:
                onward = ((1, 1, 2), (7, 2, 4))
            elif i < 4:
                onward = ((1, position + 2 if i < 3 else 7, 2),)
            elif i > 5:
                onward = ((7, position + 2, 4),)
            else:
                onward = ()
            for towards, place, number in onward:
                remote(here, here, s_plane.at[number], r_piece.at[0, place], step(towards)).start()

        def some_tokens(part):
            for k in range(1 + part, FRAMES, 8):
                other = 29 * k % FRAMES
                send_tokens(tx1, rx1, 0, (y + other // ZD) % YD, (z + other % ZD) % ZD)

        hand_on(0)
        send_x(0)
        pl.semaphore_wait(row_in, 7)
        some_tokens(0)
        for position in range(1, 8):
            some_tokens(position)
            arrived(0, position, v)
            hand_on(position)
            send_x(position)
            if position >= 3:
                forward(position - 3)
        start("q", 6)
        plane_first_wait(core, wk, 1)
        for position in range(5, 8):
            forward(position)
        start("q", 7, 8)
        for position in range(8):
            arrived(3, position, v_far)
            here = q_piece(core, -order[position] % 8, v_far)
            remote(here, here, s_span.at[0, 3], r_piece.at[4, position], (v_twin, f)).start()
        forward_moves("o")
        far_moves("o")

    @pl.when(c == 0)
    def _():
        gather(0)

    @pl.when(c == 1)
    def _():
        gather(1)

    slot_row = owners[...]
    frame_row = frame_ids[...].astype(F32)
    sub = lax.broadcasted_iota(jnp.int32, (SLOTS, SLOTS), 0)
    lane = lax.broadcasted_iota(jnp.int32, (SLOTS, SLOTS), 1)
    place = jnp.where(sub == slot_row, 1.0, 0.0)
    time_col = jnp.sum(place * frame_row, axis=1, keepdims=True)
    time_row = jnp.sum(jnp.where(sub == lane, time_col, 0.0), axis=0, keepdims=True)
    count = counts[0].astype(F32)
    distance = jnp.abs(time_col - time_row)
    valid_col = time_col < count

    for h in range(HEADS):
        bias[h // 2, :, 128 * (h % 2) : 128 * (h % 2) + 128] = jnp.where(
            valid_col, -slopes[h] * distance, -1e30
        )
    row_slot = lax.broadcasted_iota(jnp.int32, (SLOTS, ROWS), 1) // POS
    slot_col = jnp.sum(
        jnp.where(sub == lane, slot_row.astype(F32), 0.0), axis=1, keepdims=True
    )
    owner = jnp.sum(
        jnp.where(row_slot == lax.broadcasted_iota(jnp.int32, (SLOTS, ROWS), 0), slot_col, 0.0),
        axis=0, keepdims=True,
    ).astype(jnp.int32)
    row_pos = lax.broadcasted_iota(jnp.int32, (1, ROWS), 1) % POS
    to_attend = row_pos * SLOTS + owner
    to_send = owner * POS + row_pos
    out_row = lax.broadcasted_iota(jnp.int32, (128, ROWS), 0)

    tokens_wait(rx1, 0)

    def k_plane(core):
        mine_k = wk.at[y, :, :, lanes(v)] if core == 0 else wk.at[:, z, :, lanes(v)]
        for i in NEAR:
            remote(mine_k, mine_k, s_plane.at[3], r_plane.at[3],
                   along_y(i) if core == 0 else along_z(i)).start()

    @pl.when(c == 0)
    def _():
        k_plane(0)

    @pl.when(c == 1)
    def _():
        k_plane(1)

    def unpack(i, carry):
        blocks = rx1[rows_at(8 * i, 8)].astype(F32)
        held[rows_at(64 * i, 64), :512] = blocks[:, :8].reshape(64, 512).astype(BF16)
        held[rows_at(64 * i, 64), 512:] = blocks[:, 8:].reshape(64, 512).astype(BF16)
        return carry

    lax.fori_loop(0, 8, unpack, 0)

    def place_and_norm(p, carry):
        here = rows_at(128 * p, 128)
        picked = jnp.dot(
            one_hot(out_row + p * 128, to_attend), held[...], preferred_element_type=F32
        )
        normed[here] = norm(picked, gain1[...])
        resid[here] = jnp.dot(
            one_hot(out_row + p * 128, to_send), held[...], preferred_element_type=F32
        ).astype(BF16)
        return carry

    lax.fori_loop(0, POS, place_and_norm, 0)

    for position in range(8):
        here = wq.at[0, :, :, lanes(v_twin)]
        remote(here, here, s_span.at[0, 3], r_piece.at[4, position], (v_twin, f)).wait_recv()
    arrive("q", 6, 7, 8)

    flat = wq.reshape(3 * D, D)

    def project(j, carry):
        here = rows_at(512 * j, 512)
        query = lax.dot_general(flat[here], normed[...], NT, preferred_element_type=F32)
        query_t[here] = (query.astype(BF16) * 0.125).astype(BF16)
        value = lax.dot_general(
            flat[pl.ds(pl.multiple_of(2048 + 512 * j, 512), 512)], normed[...], NT,
            preferred_element_type=F32,
        )
        value_t[here] = value.astype(BF16)
        key = lax.dot_general(
            normed[...], flat[pl.ds(pl.multiple_of(1024 + 512 * j, 512), 512)], NT,
            preferred_element_type=F32,
        )
        keyed[:, rows_at(512 * j, 512)] = key.astype(BF16)
        return carry

    lax.fori_loop(0, 2, project, 0)
    span = wk.at[pl.ds(0, 7), :, :, lanes(v)]
    remote(span, span, s_plane.at[3], r_plane.at[3], (v, f)).wait_recv()
    own_moves("k")

    blank = jnp.zeros((64, 128), BF16)
    ones = jnp.ones((16, 128), BF16)

    def attend(p, carry):
        here = rows_at(SLOTS * p, SLOTS)
        for pair in range(8):
            top, bottom = pl.ds(128 * pair, 64), pl.ds(128 * pair + 64, 64)
            queries = jnp.concatenate([
                jnp.concatenate([query_t[top, here], blank], axis=1),
                jnp.concatenate([blank, query_t[bottom, here]], axis=1),
            ], axis=0)
            scores = jnp.dot(
                keyed[here, 128 * pair : 128 * pair + 128], queries, preferred_element_type=F32
            ) + bias[pair]
            expo = jnp.exp(scores - jnp.max(scores, axis=0, keepdims=True)).astype(BF16)
            values = jnp.concatenate([value_t[pl.ds(128 * pair, 128), here], ones], axis=0)
            summed = jnp.dot(values, expo, preferred_element_type=F32)
            scale = 1.0 / summed[128:129]
            attended_t[top, here] = (summed[:64, :128] * scale[:, :128]).astype(BF16)
            attended_t[bottom, here] = (summed[64:128, 128:] * scale[:, 128:]).astype(BF16)
        return carry

    lax.fori_loop(0, POS, attend, 0)
    twin_moves("o")

    column = lax.broadcasted_iota(jnp.int32, (1, ROWS), 1)
    from_attend = (column % SLOTS) * POS + column // SLOTS

    for i in range(4):
        quarter = (y // 2 + i) % 4
        here = rows_at(128 * quarter, 128)
        moved = lax.dot_general(
            one_hot(out_row + 128 * quarter, from_attend), attended_t[...], NT,
            preferred_element_type=F32,
        ).astype(BF16)
        added = jnp.dot(moved, wo[...], preferred_element_type=F32)
        both = (resid[here].astype(F32) + added).reshape(16, 8, D)
        halves = jnp.concatenate([both[:, :, :512], both[:, :, 512:]], axis=1)
        tx2[rows_at(16 * quarter, 16)] = halves.astype(BF16)
        for k in range(8):
            to_z = (z + k) % ZD
            if i == 0:
                if k:
                    send_tokens(tx2, rx2, 1, y, to_z)
                send_tokens(tx2, rx2, 1, y // 2 * 2 + 1 - y % 2, to_z)
            else:
                send_tokens(tx2, rx2, 1, 2 * quarter, to_z)
                send_tokens(tx2, rx2, 1, 2 * quarter + 1, to_z)

    rx2[f] = tx2[f]
    forward_moves("k")
    far_moves("k")
    twin_moves("k")
    tokens_wait(rx2, 1)

    def norm_arrived(i, carry):
        blocks = rx2[rows_at(16 * i, 16)].astype(F32)
        both = jnp.concatenate([blocks[:, :8], blocks[:, 8:]], axis=2).reshape(8, 2, 8, D)
        even, odd = both[:, 0], both[:, 1]
        first = jnp.where(low, even, pltpu.roll(odd, 4, 1)).reshape(64, D)
        second = jnp.where(low, pltpu.roll(even, 4, 1), odd).reshape(64, D)
        normed[rows_at(64 * i, 64)] = norm(first, gain2[...])
        normed[rows_at(256 + 64 * i, 64)] = norm(second, gain2[...])
        return carry

    lax.fori_loop(0, 4, norm_arrived, 0)

    kept = jnp.where(valid_col, 1.0, 0.0)
    slot_sub = lax.broadcasted_iota(jnp.int32, (SLOTS, 1), 0)
    kept_first = jnp.sum(jnp.where(slot_sub == 2 * f, kept, 0.0), axis=0, keepdims=True)
    kept_second = jnp.sum(jnp.where(slot_sub == 2 * f + 1, kept, 0.0), axis=0, keepdims=True)
    row_kept = jnp.where(
        lax.broadcasted_iota(jnp.int32, (ROWS, 1), 0) < 256, kept_first, kept_second
    ) > 0.5

    for j in range(4):
        weight = wk[pl.ds(2 * j, 2)].reshape(512, D)
        result = lax.dot_general(normed[...], weight, NT, preferred_element_type=F32)
        result = jnp.where(row_kept, result, 0.0).astype(BF16)
        out = keys_out if j < 2 else values_out
        out[:, pl.ds(512 * (j % 2), 512)] = result

    def sent(span, semaphore):
        remote(span, span, semaphore, r_plane.at[0], (v, f)).wait_send()

    for name, numbers in (("q", (6, 7, 8)), ("o", range(11)), ("k", range(11))):
        for number in numbers:
            move(name, number).wait_send()
    for number in range(4):
        sent(whole(wq, v), s_span.at[0, number])
    sent(wq.at[0, pl.ds(0, 7), :, lanes(v)], s_plane.at[0])
    sent(wk.at[0, pl.ds(0, 7), :, lanes(v)], s_plane.at[1])
    sent(wq.at[pl.ds(0, 4), :, :, lanes(v)], s_plane.at[2])
    sent(wq.at[pl.ds(0, 3), :, :, lanes(v)], s_plane.at[4])
    sent(wk.at[pl.ds(0, 7), :, :, lanes(v)], s_plane.at[3])
    for number in range(2):
        sent(rx1.at[pl.ds(0, FRAMES - 1)], s_tokens.at[number])


def body(tokens, counts, frame_index, owner_slot, gain_attn, gain_kv, slopes, w_qkv, w_out, w_kv):
    vmem = pl.BlockSpec(memory_space=pltpu.VMEM)
    smem = pl.BlockSpec(memory_space=pltpu.SMEM)
    dma = pltpu.SemaphoreType.DMA
    keys, values = pl.pallas_call(
        kernel,
        out_shape=(
            jax.ShapeDtypeStruct((ROWS, D), BF16),
            jax.ShapeDtypeStruct((ROWS, D), BF16),
        ),
        in_specs=[vmem] * 4 + [smem] + [vmem] * 4 + [smem],
        out_specs=(vmem, vmem),
        scratch_shapes=[
            pltpu.VMEM((YD, ZD, 48, D), BF16),
            pltpu.VMEM((YD, ZD, 32, D), BF16),
            pltpu.VMEM((D, D), BF16),
            *[pltpu.VMEM((FRAMES, 16, 512), BF16) for _ in range(4)],
            pltpu.VMEM((ROWS, D), BF16),
            pltpu.VMEM((ROWS, D), BF16),
            pltpu.VMEM((ROWS, D), BF16),
            pltpu.VMEM((D, ROWS), BF16),
            pltpu.VMEM((ROWS, D), BF16),
            pltpu.VMEM((D, ROWS), BF16),
            pltpu.VMEM((D, ROWS), BF16),
            pltpu.VMEM((8, SLOTS, 256), F32),
            pltpu.VMEM((48, 128), BF16),
            pltpu.VMEM((32, 128), BF16),
            dma((5,)), dma((4,)), dma((5, 8)), dma((3, 11)), dma((3, 11)), dma((2,)), dma((2,)),
            pltpu.SemaphoreType.REGULAR,
        ],
        compiler_params=pltpu.CompilerParams(
            collective_id=0, has_side_effects=True, vmem_limit_bytes=60 * 2**20
        ),
    )(
        tokens[0], w_qkv.T, w_kv.T, w_out, counts, frame_index, owner_slot,
        gain_attn.reshape(1, D), gain_kv.reshape(1, D), slopes,
    )
    return keys.reshape(1, 2, 256, D), values.reshape(1, 2, 256, D)


def solution(mesh):
    return jax.shard_map(
        body,
        mesh=mesh,
        in_specs=(
            P("video", "frame", None, None),
            P("video"),
            P("video", None),
            P("video", None),
            P(),
            P(),
            P(),
            P("video", "frame"),
            P(None, "video"),
            P(None, "frame"),
        ),
        out_specs=(P("video", "frame", None, None), P("video", "frame", None, None)),
        check_vma=False,
    )
```

time: 154 us -> 115 us (0.75); the launches traced: 151 us -> 115 us
  Pallas kernels: 145 us -> 110 us
    pallas_call x1, Pallas kernels: 145 us -> 110 us  [body(): pl.pallas_call(kernel, out_shape=(jax.ShapeDtypeStruct((ROWS, D), BF16),...]
    unnamed x6 -> x4, local copies, waits for them, and re-layouts: 3.48 us -> 3.32 us
where the time goes in v3:
time: 115 us
  Pallas kernels  110 us (96%)
  local copies, waits for them, and re-layouts  3.32 us (3%)
  between operations  1.3 us (1%)
    pallas_call x1, Pallas kernels, body(): pl.pallas_call(kernel, out_shape=(jax.ShapeDtypeStruct((ROWS, D), BF16),...  110 us
    unnamed x4, local copies, waits for them, and re-layouts  3.32 us

profile of v3, /device:TPU:1, one launch (start us, length us, event | category | flops | bytes accessed | tf_op | source)
XLA Modules:
  0.0 114.5 jit_solution(691682012498088009)
XLA Ops:
  1.3 109.9 %shard_map.113 = (bf16[512,1024]{1,0:T(8,128)(2,1)}, bf16[512,1024]{1,0:T(8,128)(2,1)}) custom-call(bf16[2,256,1024]{2,1,0:T(8,128)(2,1)} %bitcast.7, bf16[48,128]{1,0:T(8,128)(2,1)} %bitcast.11, bf16[32,1024]{1,0:T(8,128)(2,1)} %bitcast.10, bf16[1024,128]{1,0:T(8,128)(2,1)} %wo_mine.1, s32[1]{0:T(128)S(6)} %copy.14.counts, s32[1,128]{1,0:T(1,128)} %frame_ids.1, ...), custom_call_target="tpu_custom_call" | custom-call | tf_op jit(solution)/shard_map/pallas_call | solution.py:466
  111.2 0.0 copy-start
  111.2 2.4 %copy.15 = bf16[1,2,256,1024]{3,2,1,0:T(8,128)(2,1)} copy(bf16[1,2,256,1024]{3,2,1,0:T(8,128)(2,1)} %bitcast.9) | data formatting | bytes 2097152
  113.6 0.0 copy-done
  113.6 1.0 copy.16
Async XLA Ops:
  111.2 2.4 %copy-start = (bf16[512,1024]{1,0:T(8,128)(2,1)S(1)}, bf16[512,1024]{1,0:T(8,128)(2,1)}, u32[]{:S(2)}) copy-start(bf16[512,1024]{1,0:T(8,128)(2,1)} %get-tuple-element.5) | copy-start | bytes 3145732

commit v4 on v3

--- a/solution.py
+++ b/solution.py
@@ -14,6 +14,11 @@
 D = 1024
 HEADS = 16
 NEAR = (1, 7, 2, 6, 3, 5, 4)
+STEPS = sorted(
+    range(1, FRAMES), key=lambda k: min(k // ZD, YD - k // ZD) + min(k % ZD, ZD - k % ZD)
+)
+TURNS = [k for pair in zip(STEPS[::-1], STEPS) for k in pair][: FRAMES - 1]
+VMEM_MIB = 60
 MESH = pl.DeviceIdType.MESH
 NT = (((1,), (1,)), ((), ()))
 F32 = jnp.float32
@@ -43,8 +48,8 @@
     tok, wq_mine, wk_mine, wo_mine, counts, frame_ids, owners, gain1, gain2, slopes,
     keys_out, values_out,
     wq, wk, wo, tx1, rx1, tx2, rx2, held, resid, normed, query_t, keyed, value_t,
-    attended_t, bias, own_q, own_k,
-    s_plane, r_plane, r_piece, s_span, r_span, s_tokens, r_tokens, row_in,
+    attended_t, bias, own_q, own_k, part_q, part_k, part_v,
+    s_plane, r_plane, r_piece, s_span, r_span, s_tokens, r_tokens, r_quarter, row_in,
 ):
     v = lax.axis_index("video")
     f = lax.axis_index("frame")
@@ -75,9 +80,9 @@
 
     own_q[...] = wq_mine[...]
     own_k[...] = wk_mine[:, lanes(v)]
-    wq[y, z, :, lanes(v)] = own_q[...]
-    wk[y, z, :, lanes(v)] = own_k[...]
-    wo[:, lanes(v)] = wo_mine[...]
+    wq[v, y, z] = own_q[...]
+    wk[v, y, z] = own_k[...]
+    wo[v] = wo_mine[...]
     low = lax.broadcasted_iota(jnp.int32, (8, 8, D), 1) < 4
 
     def lay_out(i, carry):
@@ -98,27 +103,27 @@
 
     def q_piece(core, i, block):
         if core == 0:
-            return wq.at[(y + i) % YD, :, :, lanes(block)]
-        return wq.at[:, (z + i) % ZD, :, lanes(block)]
+            return wq.at[block, (y + i) % YD]
+        return wq.at[block, :, (z + i) % ZD]
 
     def whole(ref, block):
-        return ref.at[:, lanes(block)] if ref is wo else ref.at[:, :, :, lanes(block)]
+        return ref.at[block]
 
     def half(ref, number, block):
         if ref is wo:
-            return wo.at[pl.ds(512 * number, 512), lanes(block)]
-        return ref.at[pl.ds(4 * number, 4), :, :, lanes(block)]
+            return wo.at[block, pl.ds(512 * number, 512)]
+        return ref.at[block, pl.ds(4 * number, 4)]
 
     def plane_first(core, ref, mine, number):
-        here = ref.at[y, z, :, lanes(v)]
+        here = ref.at[v, y, z]
         for i in NEAR:
             remote(mine, here, s_plane.at[number], r_plane.at[number],
                    along_z(i) if core == 0 else along_y(i)).start()
 
     def seven(core, ref):
         if core == 0:
-            return ref.at[0, pl.ds(0, 7), :, lanes(v)]
-        return ref.at[pl.ds(0, 7), 0, :, lanes(v)]
+            return ref.at[v, 0, pl.ds(0, 7)]
+        return ref.at[v, pl.ds(0, 7), 0]
 
     def plane_first_wait(core, ref, number):
         span = seven(core, ref)
@@ -127,6 +132,10 @@
     def send_tokens(src, dst, number, to_y, to_z):
         g = to_y * ZD + to_z
         remote(src.at[g], dst.at[f], s_tokens.at[number], r_tokens.at[number], (v, g)).start()
+
+    def send_updated(to_y, to_z):
+        g = to_y * ZD + to_z
+        remote(tx2.at[g], rx2.at[f], s_tokens.at[1], r_quarter.at[y // 2], (v, g)).start()
 
     def tokens_wait(dst, number):
         span = dst.at[pl.ds(0, FRAMES - 1)]
@@ -232,8 +241,7 @@
                 remote(here, here, s_plane.at[number], r_piece.at[0, place], step(towards)).start()
 
         def some_tokens(part):
-            for k in range(1 + part, FRAMES, 8):
-                other = 29 * k % FRAMES
+            for other in TURNS[8 * part : 8 * part + 8]:
                 send_tokens(tx1, rx1, 0, (y + other // ZD) % YD, (z + other % ZD) % ZD)
 
         hand_on(0)
@@ -245,6 +253,8 @@
             arrived(0, position, v)
             hand_on(position)
             send_x(position)
+            if position == 5:
+                forward_moves("o")
             if position >= 3:
                 forward(position - 3)
         start("q", 6)
@@ -252,12 +262,7 @@
         for position in range(5, 8):
             forward(position)
         start("q", 7, 8)
-        for position in range(8):
-            arrived(3, position, v_far)
-            here = q_piece(core, -order[position] % 8, v_far)
-            remote(here, here, s_span.at[0, 3], r_piece.at[4, position], (v_twin, f)).start()
-        forward_moves("o")
-        far_moves("o")
+        pass
 
     @pl.when(c == 0)
     def _():
@@ -266,6 +271,12 @@
     @pl.when(c == 1)
     def _():
         gather(1)
+
+    def far_pieces(core):
+        for position in range(8):
+            here = q_piece(core, -((0,) + NEAR)[position] % 8, v_far)
+            remote(here, here, s_span.at[0, 0], r_piece.at[3, position], (v, f)).wait_recv()
+            remote(here, here, s_span.at[0, 3], r_piece.at[4, position], (v_twin, f)).start()
 
     slot_row = owners[...]
     frame_row = frame_ids[...].astype(F32)
@@ -298,7 +309,7 @@
     tokens_wait(rx1, 0)
 
     def k_plane(core):
-        mine_k = wk.at[y, :, :, lanes(v)] if core == 0 else wk.at[:, z, :, lanes(v)]
+        mine_k = wk.at[v, y] if core == 0 else wk.at[v, :, z]
         for i in NEAR:
             remote(mine_k, mine_k, s_plane.at[3], r_plane.at[3],
                    along_y(i) if core == 0 else along_z(i)).start()
@@ -332,31 +343,66 @@
 
     lax.fori_loop(0, POS, place_and_norm, 0)
 
+    arrive("q", 6, 7, 8)
+    flat = wq.reshape(8, 3 * D, 128)
+    near = (2 * x, 2 * x + 1, 2 * x_prev, 2 * x_prev + 1, 2 * x_next, 2 * x_next + 1)
+    far = (2 * x_far, 2 * x_far + 1)
+
+    def features(blocks):
+        return jnp.concatenate([normed[:, lanes(block)] for block in blocks], axis=1)
+
+    def weights_rows(start, j, blocks):
+        here = pl.ds(pl.multiple_of(start + 512 * j, 512), 512)
+        return jnp.concatenate([flat[block, here] for block in blocks], axis=1)
+
+    def project_near(j, carry):
+        here = rows_at(512 * j, 512)
+        rows = features(near)
+        part_q[here] = lax.dot_general(
+            weights_rows(0, j, near), rows, NT, preferred_element_type=F32
+        )
+        part_v[here] = lax.dot_general(
+            weights_rows(2048, j, near), rows, NT, preferred_element_type=F32
+        )
+        part_k[:, here] = lax.dot_general(
+            rows, weights_rows(1024, j, near), NT, preferred_element_type=F32
+        )
+        return carry
+
+    lax.fori_loop(0, 2, project_near, 0)
+
+    @pl.when(c == 0)
+    def _():
+        far_pieces(0)
+
+    @pl.when(c == 1)
+    def _():
+        far_pieces(1)
+
     for position in range(8):
-        here = wq.at[0, :, :, lanes(v_twin)]
+        here = wq.at[v_twin, 0]
         remote(here, here, s_span.at[0, 3], r_piece.at[4, position], (v_twin, f)).wait_recv()
-    arrive("q", 6, 7, 8)
-
-    flat = wq.reshape(3 * D, D)
 
     def project(j, carry):
         here = rows_at(512 * j, 512)
-        query = lax.dot_general(flat[here], normed[...], NT, preferred_element_type=F32)
+        rows = features(far)
+        query = part_q[here] + lax.dot_general(
+            weights_rows(0, j, far), rows, NT, preferred_element_type=F32
+        )
         query_t[here] = (query.astype(BF16) * 0.125).astype(BF16)
-        value = lax.dot_general(
-            flat[pl.ds(pl.multiple_of(2048 + 512 * j, 512), 512)], normed[...], NT,
-            preferred_element_type=F32,
+        value = part_v[here] + lax.dot_general(
+            weights_rows(2048, j, far), rows, NT, preferred_element_type=F32
         )
         value_t[here] = value.astype(BF16)
-        key = lax.dot_general(
-            normed[...], flat[pl.ds(pl.multiple_of(1024 + 512 * j, 512), 512)], NT,
-            preferred_element_type=F32,
-        )
-        keyed[:, rows_at(512 * j, 512)] = key.astype(BF16)
+        key = part_k[:, here] + lax.dot_general(
+            rows, weights_rows(1024, j, far), NT, preferred_element_type=F32
+        )
+        keyed[:, here] = key.astype(BF16)
         return carry
 
     lax.fori_loop(0, 2, project, 0)
-    span = wk.at[pl.ds(0, 7), :, :, lanes(v)]
+    far_moves("o")
+    span = wk.at[v, pl.ds(0, 7)]
     remote(span, span, s_plane.at[3], r_plane.at[3], (v, f)).wait_recv()
     own_moves("k")
 
@@ -395,7 +441,8 @@
             one_hot(out_row + 128 * quarter, from_attend), attended_t[...], NT,
             preferred_element_type=F32,
         ).astype(BF16)
-        added = jnp.dot(moved, wo[...], preferred_element_type=F32)
+        out_weight = jnp.concatenate([wo[block] for block in range(8)], axis=1)
+        added = jnp.dot(moved, out_weight, preferred_element_type=F32)
         both = (resid[here].astype(F32) + added).reshape(16, 8, D)
         halves = jnp.concatenate([both[:, :, :512], both[:, :, 512:]], axis=1)
         tx2[rows_at(16 * quarter, 16)] = halves.astype(BF16)
@@ -403,44 +450,43 @@
             to_z = (z + k) % ZD
             if i == 0:
                 if k:
-                    send_tokens(tx2, rx2, 1, y, to_z)
-                send_tokens(tx2, rx2, 1, y // 2 * 2 + 1 - y % 2, to_z)
+                    send_updated(y, to_z)
+                send_updated(y // 2 * 2 + 1 - y % 2, to_z)
             else:
-                send_tokens(tx2, rx2, 1, 2 * quarter, to_z)
-                send_tokens(tx2, rx2, 1, 2 * quarter + 1, to_z)
+                send_updated(2 * quarter, to_z)
+                send_updated(2 * quarter + 1, to_z)
 
     rx2[f] = tx2[f]
     forward_moves("k")
     far_moves("k")
     twin_moves("k")
-    tokens_wait(rx2, 1)
-
-    def norm_arrived(i, carry):
-        blocks = rx2[rows_at(16 * i, 16)].astype(F32)
-        both = jnp.concatenate([blocks[:, :8], blocks[:, 8:]], axis=2).reshape(8, 2, 8, D)
-        even, odd = both[:, 0], both[:, 1]
-        first = jnp.where(low, even, pltpu.roll(odd, 4, 1)).reshape(64, D)
-        second = jnp.where(low, pltpu.roll(even, 4, 1), odd).reshape(64, D)
-        normed[rows_at(64 * i, 64)] = norm(first, gain2[...])
-        normed[rows_at(256 + 64 * i, 64)] = norm(second, gain2[...])
-        return carry
-
-    lax.fori_loop(0, 4, norm_arrived, 0)
-
     kept = jnp.where(valid_col, 1.0, 0.0)
     slot_sub = lax.broadcasted_iota(jnp.int32, (SLOTS, 1), 0)
     kept_first = jnp.sum(jnp.where(slot_sub == 2 * f, kept, 0.0), axis=0, keepdims=True)
     kept_second = jnp.sum(jnp.where(slot_sub == 2 * f + 1, kept, 0.0), axis=0, keepdims=True)
     row_kept = jnp.where(
-        lax.broadcasted_iota(jnp.int32, (ROWS, 1), 0) < 256, kept_first, kept_second
+        lax.broadcasted_iota(jnp.int32, (128, 1), 0) < 64, kept_first, kept_second
     ) > 0.5
 
-    for j in range(4):
-        weight = wk[pl.ds(2 * j, 2)].reshape(512, D)
-        result = lax.dot_general(normed[...], weight, NT, preferred_element_type=F32)
-        result = jnp.where(row_kept, result, 0.0).astype(BF16)
-        out = keys_out if j < 2 else values_out
-        out[:, pl.ds(512 * (j % 2), 512)] = result
+    for i in range(4):
+        quarter = (y // 2 + 4 - i) % 4
+        span = rx2.at[pl.ds(0, 15 if i == 0 else 16)]
+        remote(span, span, s_tokens.at[1], r_quarter.at[quarter], (v, f)).wait_recv()
+        blocks = rx2[rows_at(16 * quarter, 16)].astype(F32)
+        both = jnp.concatenate([blocks[:, :8], blocks[:, 8:]], axis=2).reshape(8, 2, 8, D)
+        even, odd = both[:, 0], both[:, 1]
+        first = jnp.where(low, even, pltpu.roll(odd, 4, 1)).reshape(64, D)
+        second = jnp.where(low, pltpu.roll(even, 4, 1), odd).reshape(64, D)
+        rows = norm(jnp.concatenate([first, second], axis=0), gain2[...])
+        for j in range(4):
+            weight = jnp.concatenate(
+                [wk[block, pl.ds(2 * j, 2)].reshape(512, 128) for block in range(8)], axis=1
+            )
+            result = lax.dot_general(rows, weight, NT, preferred_element_type=F32)
+            result = jnp.where(row_kept, result, 0.0).astype(BF16)
+            out = keys_out if j < 2 else values_out
+            out[rows_at(64 * quarter, 64), pl.ds(512 * (j % 2), 512)] = result[:64]
+            out[pl.ds(pl.multiple_of(256 + 64 * quarter, 64), 64), pl.ds(512 * (j % 2), 512)] = result[64:]
 
     def sent(span, semaphore):
         remote(span, span, semaphore, r_plane.at[0], (v, f)).wait_send()
@@ -450,11 +496,11 @@
             move(name, number).wait_send()
     for number in range(4):
         sent(whole(wq, v), s_span.at[0, number])
-    sent(wq.at[0, pl.ds(0, 7), :, lanes(v)], s_plane.at[0])
-    sent(wk.at[0, pl.ds(0, 7), :, lanes(v)], s_plane.at[1])
-    sent(wq.at[pl.ds(0, 4), :, :, lanes(v)], s_plane.at[2])
-    sent(wq.at[pl.ds(0, 3), :, :, lanes(v)], s_plane.at[4])
-    sent(wk.at[pl.ds(0, 7), :, :, lanes(v)], s_plane.at[3])
+    sent(wq.at[v, 0, pl.ds(0, 7)], s_plane.at[0])
+    sent(wk.at[v, 0, pl.ds(0, 7)], s_plane.at[1])
+    sent(wq.at[v, pl.ds(0, 4)], s_plane.at[2])
+    sent(wq.at[v, pl.ds(0, 3)], s_plane.at[4])
+    sent(wk.at[v, pl.ds(0, 7)], s_plane.at[3])
     for number in range(2):
         sent(rx1.at[pl.ds(0, FRAMES - 1)], s_tokens.at[number])
 
@@ -472,9 +518,9 @@
         in_specs=[vmem] * 4 + [smem] + [vmem] * 4 + [smem],
         out_specs=(vmem, vmem),
         scratch_shapes=[
-            pltpu.VMEM((YD, ZD, 48, D), BF16),
-            pltpu.VMEM((YD, ZD, 32, D), BF16),
-            pltpu.VMEM((D, D), BF16),
+            pltpu.VMEM((8, YD, ZD, 48, 128), BF16),
+            pltpu.VMEM((8, YD, ZD, 32, 128), BF16),
+            pltpu.VMEM((8, D, 128), BF16),
             *[pltpu.VMEM((FRAMES, 16, 512), BF16) for _ in range(4)],
             pltpu.VMEM((ROWS, D), BF16),
             pltpu.VMEM((ROWS, D), BF16),
@@ -486,11 +532,14 @@
             pltpu.VMEM((8, SLOTS, 256), F32),
             pltpu.VMEM((48, 128), BF16),
             pltpu.VMEM((32, 128), BF16),
-            dma((5,)), dma((4,)), dma((5, 8)), dma((3, 11)), dma((3, 11)), dma((2,)), dma((2,)),
+            pltpu.VMEM((D, ROWS), F32),
+            pltpu.VMEM((ROWS, D), F32),
+            pltpu.VMEM((D, ROWS), F32),
+            dma((5,)), dma((4,)), dma((5, 8)), dma((3, 11)), dma((3, 11)), dma((2,)), dma((1,)), dma((4,)),
             pltpu.SemaphoreType.REGULAR,
         ],
         compiler_params=pltpu.CompilerParams(
-            collective_id=0, has_side_effects=True, vmem_limit_bytes=60 * 2**20
+            collective_id=0, has_side_effects=True, vmem_limit_bytes=VMEM_MIB * 2**20
         ),
     )(
         tokens[0], w_qkv.T, w_kv.T, w_out, counts, frame_index, owner_slot,

time: 115 us -> 109 us (0.948)
  Pallas kernels: 110 us -> 104 us
    pallas_call x1, Pallas kernels: 110 us -> 104 us  [body(): pl.pallas_call(kernel, out_shape=(jax.ShapeDtypeStruct((ROWS, D), BF16),...]
where the time goes in v4:
time: 109 us
  Pallas kernels  104 us (95%)
  local copies, waits for them, and re-layouts  3.32 us (3%)
  between operations  1.3 us (1%)
    pallas_call x1, Pallas kernels, body(): pl.pallas_call(kernel, out_shape=(jax.ShapeDtypeStruct((ROWS, D), BF16),...  104 us
    unnamed x4, local copies, waits for them, and re-layouts  3.32 us

profile of v4, /device:TPU:1, one launch (start us, length us, event | category | flops | bytes accessed | tf_op | source)
XLA Modules:
  0.0 108.7 jit_solution(9567631874975839218)
XLA Ops:
  1.3 104.0 %shard_map.113 = (bf16[512,1024]{1,0:T(8,128)(2,1)}, bf16[512,1024]{1,0:T(8,128)(2,1)}) custom-call(bf16[2,256,1024]{2,1,0:T(8,128)(2,1)} %bitcast.7, bf16[48,128]{1,0:T(8,128)(2,1)} %bitcast.11, bf16[32,1024]{1,0:T(8,128)(2,1)} %bitcast.10, bf16[1024,128]{1,0:T(8,128)(2,1)} %wo_mine.1, s32[1]{0:T(128)S(6)} %copy.14.counts, s32[1,128]{1,0:T(1,128)} %frame_ids.1, ...), custom_call_target="tpu_custom_call" | custom-call | tf_op jit(solution)/shard_map/pallas_call | solution.py:512
  105.3 0.0 copy-start
  105.3 2.4 %copy.15 = bf16[1,2,256,1024]{3,2,1,0:T(8,128)(2,1)} copy(bf16[1,2,256,1024]{3,2,1,0:T(8,128)(2,1)} %bitcast.9) | data formatting | bytes 2097152
  107.7 0.0 copy-done
  107.7 1.0 copy.16
Async XLA Ops:
  105.3 2.4 %copy-start = (bf16[512,1024]{1,0:T(8,128)(2,1)S(1)}, bf16[512,1024]{1,0:T(8,128)(2,1)}, u32[]{:S(2)}) copy-start(bf16[512,1024]{1,0:T(8,128)(2,1)} %get-tuple-element.5) | copy-start | bytes 3145732

commit v5 on v4

--- a/solution.py
+++ b/solution.py
@@ -45,10 +45,10 @@
 
 
 def kernel(
-    tok, wq_mine, wk_mine, wo_mine, counts, frame_ids, owners, gain1, gain2, slopes,
+    tok_in, wq_mine, wk_mine, wo_mine, counts, frame_ids, owners, gain1, gain2, slopes,
     keys_out, values_out,
     wq, wk, wo, tx1, rx1, tx2, rx2, held, resid, normed, query_t, keyed, value_t,
-    attended_t, bias, own_q, own_k, part_q, part_k, part_v,
+    attended_t, bias, tok, own, part_q, part_k, part_v,
     s_plane, r_plane, r_piece, s_span, r_span, s_tokens, r_tokens, r_quarter, row_in,
 ):
     v = lax.axis_index("video")
@@ -71,6 +71,16 @@
     def along_z(i):
         return (v, y * ZD + (z + i) % ZD)
 
+    loads = [
+        pltpu.make_async_copy(src, dst, own.at[number])
+        for number, (src, dst) in enumerate((
+            (wq_mine, wq.at[v, y, z]), (wk_mine.at[:, lanes(v)], wk.at[v, y, z]),
+            (wo_mine, wo.at[v]), (tok_in, tok),
+        ))
+    ]
+    for load in loads:
+        load.start()
+
     barrier = pltpu.get_barrier_semaphore()
     for i in range(1, 8):
         for device in (along_y(i), along_z(i)):
@@ -78,11 +88,8 @@
     for other in (v_next, v_prev, v_twin):
         pl.semaphore_signal(barrier, inc=1, device_id=(other, f), device_id_type=MESH)
 
-    own_q[...] = wq_mine[...]
-    own_k[...] = wk_mine[:, lanes(v)]
-    wq[v, y, z] = own_q[...]
-    wk[v, y, z] = own_k[...]
-    wo[v] = wo_mine[...]
+    for load in loads:
+        load.wait()
     low = lax.broadcasted_iota(jnp.int32, (8, 8, D), 1) < 4
 
     def lay_out(i, carry):
@@ -114,10 +121,10 @@
             return wo.at[block, pl.ds(512 * number, 512)]
         return ref.at[block, pl.ds(4 * number, 4)]
 
-    def plane_first(core, ref, mine, number):
+    def plane_first(core, ref, number):
         here = ref.at[v, y, z]
         for i in NEAR:
-            remote(mine, here, s_plane.at[number], r_plane.at[number],
+            remote(here, here, s_plane.at[number], r_plane.at[number],
                    along_z(i) if core == 0 else along_y(i)).start()
 
     def seven(core, ref):
@@ -199,8 +206,8 @@
 
     def gather(core):
         order = (0,) + NEAR
-        plane_first(core, wq, own_q, 0)
-        plane_first(core, wk, own_k, 1)
+        plane_first(core, wq, 0)
+        plane_first(core, wk, 1)
         own_moves("o")
         plane_first_wait(core, wq, 0)
 
@@ -507,15 +514,13 @@
 
 def body(tokens, counts, frame_index, owner_slot, gain_attn, gain_kv, slopes, w_qkv, w_out, w_kv):
     vmem = pl.BlockSpec(memory_space=pltpu.VMEM)
+    hbm = pl.BlockSpec(memory_space=pltpu.HBM)
     smem = pl.BlockSpec(memory_space=pltpu.SMEM)
     dma = pltpu.SemaphoreType.DMA
     keys, values = pl.pallas_call(
         kernel,
-        out_shape=(
-            jax.ShapeDtypeStruct((ROWS, D), BF16),
-            jax.ShapeDtypeStruct((ROWS, D), BF16),
-        ),
-        in_specs=[vmem] * 4 + [smem] + [vmem] * 4 + [smem],
+        out_shape=(pltpu.VMEM((ROWS, D), BF16), pltpu.VMEM((ROWS, D), BF16)),
+        in_specs=[hbm] * 4 + [smem] + [vmem] * 4 + [smem],
         out_specs=(vmem, vmem),
         scratch_shapes=[
             pltpu.VMEM((8, YD, ZD, 48, 128), BF16),
@@ -530,8 +535,8 @@
             pltpu.VMEM((D, ROWS), BF16),
             pltpu.VMEM((D, ROWS), BF16),
             pltpu.VMEM((8, SLOTS, 256), F32),
-            pltpu.VMEM((48, 128), BF16),
-            pltpu.VMEM((32, 128), BF16),
+            pltpu.VMEM((2, 256, D), BF16),
+            dma((4,)),
             pltpu.VMEM((D, ROWS), F32),
             pltpu.VMEM((ROWS, D), F32),
             pltpu.VMEM((D, ROWS), F32),

time: 109 us -> 105 us (0.963)
  Pallas kernels: 104 us -> 102 us
  local copies, waits for them, and re-layouts: 3.32 us -> 1.94 us
    pallas_call x1, Pallas kernels: 104 us -> 102 us  [body(): pl.pallas_call(kernel, out_shape=(pltpu.VMEM((ROWS, D), BF16), pltpu.VMEM...]
    unnamed x4 -> x2, local copies, waits for them, and re-layouts: 3.32 us -> 1.94 us
where the time goes in v5:
time: 105 us
  Pallas kernels  102 us (97%)
  local copies, waits for them, and re-layouts  1.94 us (2%)
  between operations  1.29 us (1%)
    pallas_call x1, Pallas kernels, body(): pl.pallas_call(kernel, out_shape=(pltpu.VMEM((ROWS, D), BF16), pltpu.VMEM...  102 us

profile of v5, /device:TPU:1, one launch (start us, length us, event | category | flops | bytes accessed | tf_op | source)
XLA Modules:
  0.0 105.1 jit_solution(1237190014493867566)
XLA Ops:
  1.3 101.8 %shard_map.113 = (bf16[512,1024]{1,0:T(8,128)(2,1)S(1)}, bf16[512,1024]{1,0:T(8,128)(2,1)S(1)}) custom-call(bf16[2,256,1024]{2,1,0:T(8,128)(2,1)} %bitcast.9, bf16[48,128]{1,0:T(8,128)(2,1)} %bitcast.11, bf16[32,1024]{1,0:T(8,128)(2,1)} %bitcast.10, bf16[1024,128]{1,0:T(8,128)(2,1)} %wo_mine.1, s32[1]{0:T(128)S(6)} %copy.16.counts, s32[1,128]{1,0:T(1,128)} %frame_ids.1, ...), custom_call_target="tpu_custom_call" | custom-call | tf_op jit(solution)/shard_map/pallas_call | solution.py:520
  103.1 1.0 copy.14
  104.1 1.0 copy.15
